TPU v7x, 32 devices: a whole 2x2x4 slice. The times are simulated.
32 devices in a mesh: wide: 16 (over z, x, core), narrow: 2 (over y).
Axes of the slice: x: 2, y: 2, z: 4, core: 2. Of those that a mesh axis runs over, the one named last changes fastest.
Arguments:
- inputs: bfloat16 [64, 512, 512], P('wide', 'narrow'), may hold values from -12 to 12
- cotangent: bfloat16 [64, 512, 512], P('wide', 'narrow'), may hold values from -6 to 6
- ln1_gain: bfloat16 [512], replicated, may hold values from 0.5 to 1.5
- w_qkv: bfloat16 [512, 1536], replicated, may hold values from -0.25 to 0.25
- w_attn_out: bfloat16 [512, 512], replicated, may hold values from -3.5 to 3.5
- ln2_gain: bfloat16 [512], replicated, may hold values from 0.5 to 1.5
- w_router: bfloat16 [512, 16], replicated, may hold values from -0.1875 to 0.1875
- expert_in: bfloat16 [16, 512, 2048], P('wide'), may hold values from -0.25 to 0.25
- expert_in_bias: bfloat16 [16, 2048], P('wide'), may hold values from -0.59765625 to 0.59765625
- expert_out: bfloat16 [16, 2048, 512], P('wide'), may hold values from -1.75 to 1.75
- expert_out_bias: bfloat16 [16, 512], P('wide'), may hold values from -4.78125 to 4.78125
- route_ids: int32 [64, 512, 2], P('wide', 'narrow'), may hold values from 0 to 15, as said below
- route_slots: int32 [64, 512, 2], P('wide', 'narrow'), may hold values from 0 to 133, as said below
- route_dropped: int32 [64, 512, 2], P('wide', 'narrow'), may hold values from 0 to 1, as said below
Outputs:
- block_out: bfloat16 [64, 512, 512], P('wide', 'narrow')
- input_grad: float32 [64, 512, 512], P('wide', 'narrow')
- grad_ln1_gain: float32 [512], replicated
- grad_qkv: float32 [512, 1536], replicated
- grad_attn_out: float32 [512, 512], replicated
- grad_ln2_gain: float32 [512], replicated
- grad_router: float32 [512, 16], replicated
- grad_expert_in: float32 [16, 512, 2048], P('wide')
- grad_expert_in_bias: float32 [16, 2048], P('wide')
- grad_expert_out: float32 [16, 2048, 512], P('wide')
- grad_expert_out_bias: float32 [16, 512], P('wide')
- stats: float32 [3], replicated
Inputs may be any that keep to these rules, and one draw needn't show every extreme that they name: `route_ids`: each token names two different experts. `route_slots`: among the tokens of one device, the kept pairs of one expert take distinct slots, given in priority order with all first choices before all second choices; a dropped pair carries slot 0. In every group of devices along wide with the same index of narrow, one expert has all 134 slots taken from every device. `route_dropped`: 1 exactly for the pairs that come after the 134 kept pairs of their expert among the tokens of one device.
All inputs are finite; a program needn't handle non-finite values.
Results may differ from a plain program's by a relative error of at most 0.014.
Values may be sent and summed in bfloat16 or wider, within the bound.
No kernel may reach another device: no remote copies, remote signals or barrier semaphores. Data moves between devices by JAX's collectives and lax.ppermute only.
A program may use at most 384 MiB of HBM per device.

v0:
```python
import math

import jax
import jax.numpy as jnp
from jax import lax
from jax.sharding import PartitionSpec as P

HEADS = 8
TOP = 2


EPS = 1e-06


def normalize(values):
    centre = jnp.mean(values, -1, keepdims=True)
    shifted = values - centre
    inverse = lax.rsqrt(jnp.mean(shifted * shifted, -1, keepdims=True) + EPS)
    return (shifted * inverse, inverse)


def norm_back(d_normed, normed, inverse):
    return inverse * (
        d_normed
        - jnp.mean(d_normed, -1, keepdims=True)
        - normed * jnp.mean(d_normed * normed, -1, keepdims=True)
    )


def shards(
    inputs,
    cotangent,
    ln1_gain,
    w_qkv,
    w_attn_out,
    ln2_gain,
    w_router,
    expert_in,
    expert_in_bias,
    expert_out,
    expert_out_bias,
    route_ids,
    route_slots,
    route_dropped,
):
    images, rows_dev, width = inputs.shape
    tokens = images * rows_dev
    head_dim = width // HEADS
    scale = head_dim ** (-0.5)
    experts = w_router.shape[1]
    own_experts = expert_in.shape[0]
    n_wide = lax.axis_size("wide")
    n_narrow = lax.axis_size("narrow")
    seq_len = rows_dev * n_narrow
    capacity = max(2, 42 * tokens // (20 * experts))
    group = math.gcd(images, max(1, 512 // rows_dev))
    blocks = images // group
    x_float = inputs.astype(jnp.float32).reshape(tokens, width)
    gain_one = ln1_gain.astype(jnp.float32)
    gain_two = ln2_gain.astype(jnp.float32)
    normed_one, inverse_one = normalize(x_float)
    input_one = (normed_one * gain_one).astype(jnp.bfloat16)
    projected = jnp.dot(input_one, w_qkv, preferred_element_type=jnp.float32).astype(jnp.bfloat16)
    queries = projected[:, :width].reshape(images, rows_dev, width)
    keys_own = projected[:, width : 2 * width].reshape(images, rows_dev, width)
    values_own = projected[:, 2 * width :].reshape(images, rows_dev, width)
    keys_all, values_all = (
        lax.all_gather(keys_own, "narrow", axis=1, tiled=True),
        lax.all_gather(values_own, "narrow", axis=1, tiled=True),
    )
    query_blocks = queries.reshape(blocks, group, rows_dev, HEADS, head_dim)
    key_blocks = keys_all.reshape(blocks, group, seq_len, HEADS, head_dim)
    value_blocks = values_all.reshape(blocks, group, seq_len, HEADS, head_dim)

    def attend_block(operands):
        query_b, key_b, value_b = operands
        scores = (
            jnp.einsum("gqhd,gkhd->ghqk", query_b, key_b, preferred_element_type=jnp.float32)
            * scale
        )
        top_score = jnp.max(scores, -1, keepdims=True)
        exponent = jnp.exp(scores - top_score)
        total = jnp.sum(exponent, -1, keepdims=True)
        weights = (exponent / total).astype(jnp.bfloat16)
        mixed = jnp.einsum("ghqk,gkhd->gqhd", weights, value_b, preferred_element_type=jnp.float32)
        return (mixed.astype(jnp.bfloat16), (top_score + jnp.log(total))[..., 0])

    heads_out, log_total = lax.map(attend_block, (query_blocks, key_blocks, value_blocks))
    heads_flat = heads_out.reshape(tokens, width)
    attn_out = jnp.dot(heads_flat, w_attn_out, preferred_element_type=jnp.float32)
    residual = x_float + attn_out
    normed_two, inverse_two = normalize(residual)
    input_two = (normed_two * gain_two).astype(jnp.bfloat16)
    logits = jnp.dot(input_two, w_router, preferred_element_type=jnp.float32)
    top_logit = jnp.max(logits, -1, keepdims=True)
    gate_exp = jnp.exp(logits - top_logit)
    gate_probs = gate_exp / jnp.sum(gate_exp, -1, keepdims=True)
    choice_ids = route_ids.reshape(tokens, TOP)
    dropped = route_dropped.reshape(tokens, TOP)
    kept = (1 - dropped).astype(jnp.float32)
    selector = (choice_ids[:, :, None] == jnp.arange(experts, dtype=jnp.int32)).astype(jnp.float32)
    combine = jnp.sum(selector * gate_probs[:, None, :], -1) * kept
    target = jnp.where(
        dropped == 0, choice_ids * capacity + route_slots.reshape(tokens, TOP), experts * capacity
    ).reshape(-1)
    fetch = jnp.minimum(target, experts * capacity - 1)
    pair_rows = jnp.broadcast_to(input_two[:, None, :], (tokens, TOP, width)).reshape(
        tokens * TOP, width
    )
    outgoing = (
        jnp.zeros((experts * capacity, width), jnp.bfloat16).at[target].set(pair_rows, mode="drop")
    )
    outgoing = outgoing.reshape(experts, capacity, width)
    in_bias = expert_in_bias.astype(jnp.float32)
    out_bias = expert_out_bias.astype(jnp.float32)
    received = lax.all_to_all(outgoing, "wide", split_axis=0, concat_axis=0, tiled=True)
    slots_here = received.shape[1]
    arrived = received.reshape(n_wide, own_experts, slots_here, width)
    hidden_pre = (
        jnp.einsum("sxcd,xdf->sxcf", arrived, expert_in, preferred_element_type=jnp.float32)
        + in_bias[None, :, None, :]
    )
    activated = jax.nn.gelu(hidden_pre).astype(jnp.bfloat16)
    produced = (
        jnp.einsum("sxcf,xfd->sxcd", activated, expert_out, preferred_element_type=jnp.float32)
        + out_bias[None, :, None, :]
    )
    produced = produced.astype(jnp.bfloat16).reshape(n_wide * own_experts, slots_here, width)
    returned = lax.all_to_all(produced, "wide", split_axis=0, concat_axis=0, tiled=True)
    hidden_width = hidden_pre.shape[-1]
    returned, arrived_kept, hidden_kept, activated_kept = (
        returned,
        received,
        hidden_pre.reshape(n_wide * own_experts, slots_here, hidden_width),
        activated.reshape(n_wide * own_experts, slots_here, hidden_width),
    )
    picked = (
        returned.reshape(experts * capacity, width)[fetch]
        .reshape(tokens, TOP, width)
        .astype(jnp.float32)
    )
    moe_out = jnp.sum(combine[:, :, None] * picked, 1)
    block_out = (residual + moe_out).astype(jnp.bfloat16).reshape(images, rows_dev, width)
    moment_terms = jnp.stack(
        [jnp.sum(residual * residual), jnp.sum(attn_out * attn_out), jnp.sum(moe_out * moe_out)]
    )
    moment_count = tokens * width * n_wide * n_narrow
    moment_sums = lax.psum(moment_terms, ("wide", "narrow"))
    upstream = cotangent.astype(jnp.float32).reshape(tokens, width)
    d_combine = jnp.sum(upstream[:, None, :] * picked, -1) * kept
    d_gates = jnp.sum(selector * d_combine[:, :, None], 1)
    d_logits = (gate_probs * (d_gates - jnp.sum(gate_probs * d_gates, -1, keepdims=True))).astype(
        jnp.bfloat16
    )
    d_router = jnp.dot(input_two.T, d_logits, preferred_element_type=jnp.float32)
    grad_rows = (
        (combine[:, :, None] * upstream[:, None, :])
        .astype(jnp.bfloat16)
        .reshape(tokens * TOP, width)
    )
    d_outgoing = (
        jnp.zeros((experts * capacity, width), jnp.bfloat16).at[target].set(grad_rows, mode="drop")
    )
    d_outgoing = d_outgoing.reshape(experts, capacity, width)
    d_produced = lax.all_to_all(
        d_outgoing, "wide", split_axis=0, concat_axis=0, tiled=True
    ).reshape(n_wide, own_experts, capacity, width)
    hidden_width = hidden_kept.shape[-1]
    arrived_four = arrived_kept.reshape(n_wide, own_experts, capacity, width)
    hidden_four = hidden_kept.reshape(n_wide, own_experts, capacity, hidden_width)
    activated_four = activated_kept.reshape(n_wide, own_experts, capacity, hidden_width)
    d_expert_out = jnp.einsum(
        "sxcf,sxcd->xfd", activated_four, d_produced, preferred_element_type=jnp.float32
    )
    d_out_bias = jnp.sum(d_produced.astype(jnp.float32), (0, 2))
    d_activated = jnp.einsum(
        "sxcd,xfd->sxcf", d_produced, expert_out, preferred_element_type=jnp.float32
    )
    unused_value, gelu_pull = jax.vjp(jax.nn.gelu, hidden_four)
    d_hidden = gelu_pull(d_activated)[0].astype(jnp.bfloat16)
    d_expert_in = jnp.einsum(
        "sxcd,sxcf->xdf", arrived_four, d_hidden, preferred_element_type=jnp.float32
    )
    d_in_bias = jnp.sum(d_hidden.astype(jnp.float32), (0, 2))
    d_arrived = jnp.einsum(
        "sxcf,xdf->sxcd", d_hidden, expert_in, preferred_element_type=jnp.float32
    )
    d_arrived = d_arrived.astype(jnp.bfloat16).reshape(n_wide * own_experts, capacity, width)
    d_back = lax.all_to_all(d_arrived, "wide", split_axis=0, concat_axis=0, tiled=True).reshape(
        experts * capacity, width
    )
    d_pairs = d_back[fetch].reshape(tokens, TOP, width).astype(jnp.float32)
    d_input_two = jnp.sum(d_pairs * kept[:, :, None], 1) + jnp.dot(
        d_logits, w_router.T, preferred_element_type=jnp.float32
    )
    expert_sums = (
        lax.psum(d_expert_in.astype(jnp.bfloat16), "narrow").astype(jnp.float32),
        lax.psum(d_in_bias.astype(jnp.bfloat16), "narrow").astype(jnp.float32),
        lax.psum(d_expert_out.astype(jnp.bfloat16), "narrow").astype(jnp.float32),
        lax.psum(d_out_bias.astype(jnp.bfloat16), "narrow").astype(jnp.float32),
    )
    d_gain_two = jnp.sum(d_input_two * normed_two, 0)
    d_residual = upstream + norm_back(d_input_two * gain_two, normed_two, inverse_two)
    d_attn = d_residual.astype(jnp.bfloat16)
    d_attn_weight = jnp.dot(heads_flat.T, d_attn, preferred_element_type=jnp.float32)
    d_heads = jnp.dot(d_attn, w_attn_out.T, preferred_element_type=jnp.float32).astype(jnp.bfloat16)
    d_head_blocks = d_heads.reshape(blocks, group, rows_dev, HEADS, head_dim)

    def score_grads(query_b, key_b, value_b, total_b, d_head_b):
        scores = (
            jnp.einsum("gqhd,gkhd->ghqk", query_b, key_b, preferred_element_type=jnp.float32)
            * scale
        )
        weights = jnp.exp(scores - total_b[..., None])
        d_weights = jnp.einsum(
            "gqhd,gkhd->ghqk", d_head_b, value_b, preferred_element_type=jnp.float32
        )
        spread = jnp.sum(weights * d_weights, -1, keepdims=True)
        d_scores = (weights * (d_weights - spread)).astype(jnp.bfloat16)
        d_query = (
            jnp.einsum("ghqk,gkhd->gqhd", d_scores, key_b, preferred_element_type=jnp.float32)
            * scale
        )
        return (weights, d_scores, d_query.astype(jnp.bfloat16), spread[..., 0])

    def back_block(operands):
        query_b, key_b, value_b, total_b, d_head_b = operands
        weights, d_scores, d_query, spread = score_grads(query_b, key_b, value_b, total_b, d_head_b)
        d_key = (
            jnp.einsum("ghqk,gqhd->gkhd", d_scores, query_b, preferred_element_type=jnp.float32)
            * scale
        )
        d_value = jnp.einsum(
            "ghqk,gqhd->gkhd",
            weights.astype(jnp.bfloat16),
            d_head_b,
            preferred_element_type=jnp.float32,
        )
        return (d_query, d_key, d_value)

    d_queries, key_terms, value_terms = lax.map(
        back_block, (query_blocks, key_blocks, value_blocks, log_total, d_head_blocks)
    )
    key_sum, value_sum = (
        lax.psum_scatter(
            key_terms.reshape(images, seq_len, width), "narrow", scatter_dimension=1, tiled=True
        ),
        lax.psum_scatter(
            value_terms.reshape(images, seq_len, width), "narrow", scatter_dimension=1, tiled=True
        ),
    )
    d_keys = key_sum.astype(jnp.bfloat16).reshape(tokens, width)
    d_values = value_sum.astype(jnp.bfloat16).reshape(tokens, width)
    d_projected = jnp.concatenate([d_queries.reshape(tokens, width), d_keys, d_values], 1)
    d_qkv_weight = jnp.dot(input_one.T, d_projected, preferred_element_type=jnp.float32)
    d_input_one = jnp.dot(d_projected, w_qkv.T, preferred_element_type=jnp.float32)
    d_gain_one = jnp.sum(d_input_one * normed_one, 0)
    input_grad = d_residual + norm_back(d_input_one * gain_one, normed_one, inverse_one)
    dense = lax.psum(
        (d_gain_one, d_qkv_weight, d_attn_weight, d_gain_two, d_router), ("wide", "narrow")
    )
    stats = jnp.sqrt(moment_sums / moment_count + EPS)
    return (
        block_out,
        input_grad.reshape(images, rows_dev, width),
        dense[0],
        dense[1],
        dense[2],
        dense[3],
        dense[4],
        expert_sums[0],
        expert_sums[1],
        expert_sums[2],
        expert_sums[3],
        stats,
    )


def solution(mesh):
    return jax.shard_map(
        shards,
        mesh=mesh,
        in_specs=(
            P("wide", "narrow", None),
            P("wide", "narrow", None),
            P(),
            P(),
            P(),
            P(),
            P(),
            P("wide", None, None),
            P("wide", None),
            P("wide", None, None),
            P("wide", None),
            P("wide", "narrow", None),
            P("wide", "narrow", None),
            P("wide", "narrow", None),
        ),
        out_specs=(
            P("wide", "narrow", None),
            P("wide", "narrow", None),
            P(),
            P(),
            P(),
            P(),
            P(),
            P("wide", None, None),
            P("wide", None),
            P("wide", None, None),
            P("wide", None),
            P(),
        ),
        check_vma=False,
    )
```

profile of v0, /device:TPU:0, one launch (start us, length us, event | category | flops | bytes accessed | tf_op | source)
XLA Modules:
  0.0 818.1 jit_solution(13742694481632525472)
XLA Ops:
  25.1 27.6 %all-gather.3.cloned.1.call-done = bf16[4,512,512]{2,1,0:T(8,128)(2,1)} async-done(((bf16[4,256,512]{2,1,0:T(8,128)(2,1)}), bf16[4,512,512]{2,1,0:T(8,128)(2,1)}) %all-gather.3.cloned.1.call-update) | async-done | bytes 2097168 | tf_op jit(solution)/shard_map/all_gather | solution.py:69
  52.7 4.1 copy.123
  56.8 31.1 %all-gather.5.cloned.1.call-done = bf16[4,512,512]{2,1,0:T(8,128)(2,1)} async-done(((bf16[4,256,512]{2,1,0:T(8,128)(2,1)}), bf16[4,512,512]{2,1,0:T(8,128)(2,1)}) %all-gather.5.cloned.1.call-update) | async-done | bytes 2097168 | tf_op jit(solution)/shard_map/all_gather | solution.py:68
  87.9 4.2 copy.125
  93.6 17.4 %while.26 = (s32[]{:T(128)}, bf16[2,2,256,8,64]{2,1,0,4,3:T(2,128)(2,1)}, f32[2,2,8,256]{3,2,1,0:T(8,128)S(1)}, bf16[2,2,512,8,64]{2,4,3,1,0:T(8,128)(2,1)}, bf1...) while((s32[]{:T(128)}, bf16[2,2,256,8,64]{2,1,0,4,3:T(2,128)(2,1)}, ...), condition=%wide.region_5.6_spmd, body=%wide.region_2.5_spmd.sunk | while | flops 556003328 | bytes 37881456 | solution.py:88
  113.6 3.4 fusion.124
  122.1 4.1 reshape.413
  126.2 11.7 %scatter_custom_fusion = bf16[2144,512]{1,0:T(8,128)(2,1)} fusion(s32[2048]{0:T(1024)S(1)} %bitcast.311, bf16[2048,512]{1,0:T(8,128)(2,1)} %reshape.413, bf16[]{:T(256)} %constant.55.clone.1), kind=kCustom, calls=%fused_computation.139 | custom fusion | bytes 2195968 | tf_op jit(solution)/shard_map/scatter | solution.py:111
  137.9 4.0 reshape.368
  141.9 5.7 all-to-all-start
  149.9 4.3 mul.292
  154.2 6.1 mul.293
  164.4 12.5 %scatter_custom_fusion.1 = bf16[2144,512]{1,0:T(8,128)(2,1)} fusion(s32[2048]{0:T(1024)S(1)} %bitcast.312, f32[2048,512]{1,0:T(8,128)} %mul.293, f32[2048]{0:T(1024)S(1)} %mul.290, bf16[]{:T(256)} %constant.55.clone.1), kind=kCustom, calls=%fused_computation.97 | custom fusion | flops 2097152 | bytes 6397954 | tf_op jit(solution)/shard_map/scatter | solution.py:162
  176.9 4.0 reshape.377
  181.0 10.1 %all-to-all-done = bf16[16,134,512]{2,1,0:T(8,128)(2,1)} async-done(((bf16[16,134,512]{2,1,0:T(8,128)(2,1)}), bf16[16,134,512]{2,1,0:T(8,128)(2,1)}, u32[]{:S(2)}, u32[]{:S(2)}) %all-to-all-start) | async-done | bytes 2195488 | tf_op jit(solution)/shard_map/all_to_all | solution.py:116
  191.0 12.1 %all-to-all-start.2 = ((bf16[16,134,512]{2,1,0:T(8,128)(2,1)}), bf16[16,134,512]{2,1,0:T(8,128)(2,1)}, u32[]{:S(2)}, u32[]{:S(2)}) async-start(bf16[16,134,512]{2,1,0:T(8,128)(2,1)} %reshape.377), calls=%async_computation.2 | async-start | bytes 4456448 | tf_op jit(solution)/shard_map/all_to_all | solution.py:165
  203.2 7.1 fusion.82
  210.3 6.1 copy-done.55
  216.4 8.0 fusion.75
  224.4 22.1 %all-to-all-done.2 = bf16[16,134,512]{2,1,0:T(8,128)(2,1)} async-done(((bf16[16,134,512]{2,1,0:T(8,128)(2,1)}), bf16[16,134,512]{2,1,0:T(8,128)(2,1)}, u32[]{:S(2)}, u32[]{:S(2)}) %all-to-all-start.2) | async-done | bytes 2195488 | tf_op jit(solution)/shard_map/all_to_all | solution.py:165
  246.5 12.3 %all-to-all-start.1 = ((bf16[16,134,512]{2,1,0:T(8,128)(2,1)}), bf16[16,134,512]{2,1,0:T(8,128)(2,1)}, u32[]{:S(2)}, u32[]{:S(2)}) async-start(bf16[16,134,512]{2,1,0:T(8,128)(2,1)} %fusion.75), calls=%async_computation.1 | async-start | bytes 4456448 | tf_op jit(solution)/shard_map/all_to_all | solution.py:129
  258.8 20.9 %fusion.127 = (bf16[2048]{0:T(1024)(128)(2,1)}, bf16[16,1,134,2048]{3,2,0,1:T(8,128)(2,1)S(1)}) fusion(f32[2048]{0:T(1024)S(1)} %bitcast.314, f32[16,134,2048]{2,1,0:T(8,128)} %copy-done.55, bf16[16,134,512]{2,1,0:T(8,128)(2,1)} %all-to-all-done.2, bf16[1,2048,512]{2,1,0:T(8,128)(2,1)S(1)} %copy-done), kind=kOutput, calls=%fused_computation.181 | convolution fusion | flops 4592891904 | bytes 30650368 | tf_op jit(solution)/shard_map/sxcd,xfd->sxcf/dot_general | solution.py:176
  279.7 3.5 copy-done.57
  283.2 6.4 fusion.98
  289.6 12.6 %all-to-all-done.1 = bf16[16,134,512]{2,1,0:T(8,128)(2,1)} async-done(((bf16[16,134,512]{2,1,0:T(8,128)(2,1)}), bf16[16,134,512]{2,1,0:T(8,128)(2,1)}, u32[]{:S(2)}, u32[]{:S(2)}) %all-to-all-start.1) | async-done | bytes 2195488 | tf_op jit(solution)/shard_map/all_to_all | solution.py:129
  302.2 11.8 %all-to-all-start.3 = ((bf16[16,134,512]{2,1,0:T(8,128)(2,1)}), bf16[16,134,512]{2,1,0:T(8,128)(2,1)}, u32[]{:S(2)}, u32[]{:S(2)}) async-start(bf16[16,134,512]{2,1,0:T(8,128)(2,1)} %fusion.98), calls=%async_computation.3 | async-start | bytes 4456448 | tf_op jit(solution)/shard_map/all_to_all | solution.py:189
  320.6 9.2 %gather_fusion = bf16[2048,512]{1,0:T(8,128)(2,1)} fusion(bf16[2144,512]{1,0:T(8,128)(2,1)S(1)} %reshape.373, s32[2048]{0:T(1024)S(1)} %broadcast_clamp_fusion), kind=kCustom, calls=%fused_computation | custom fusion | bytes 4202496 | tf_op jit(solution)/shard_map/gather | solution.py:138
  329.8 5.6 reshape.389
  335.4 11.2 %multiply_reduce_fusion.2 = (f32[1024,2]{1,0:T(8,128)}, f32[1024,512]{1,0:T(8,128)}) fusion(f32[1024,2,512]{2,1,0:T(2,128)} %reshape.389, f32[1024,512]{1,0:T(8,128)S(1)} %copy-done.16, f32[1024,2]{1,0:T(8,128)} %copy.130), kind=kLoop, calls=%fused_computation.88 | loop fusion | flops 3667968 | bytes 8404992 | tf_op jit(solution)/shard_map/reduce_sum | solution.py:150
  348.0 9.5 %all-to-all-done.3 = bf16[16,134,512]{2,1,0:T(8,128)(2,1)} async-done(((bf16[16,134,512]{2,1,0:T(8,128)(2,1)}), bf16[16,134,512]{2,1,0:T(8,128)(2,1)}, u32[]{:S(2)}, u32[]{:S(2)}) %all-to-all-start.3) | async-done | bytes 2195488 | tf_op jit(solution)/shard_map/all_to_all | solution.py:189
  360.1 9.2 %gather_fusion.1 = bf16[2048,512]{1,0:T(8,128)(2,1)} fusion(bf16[2144,512]{1,0:T(8,128)(2,1)S(1)} %reshape.379, s32[2048]{0:T(1024)S(1)} %broadcast_clamp_fusion), kind=kCustom, calls=%fused_computation.1 | custom fusion | bytes 4202496 | tf_op jit(solution)/shard_map/gather | solution.py:192
  369.3 5.5 reshape.392
  374.8 7.7 multiply_reduce_fusion.3
  391.6 3.1 copy.138
  396.3 30.6 %while.27 = (s32[]{:T(128)}, bf16[2,2,256,8,64]{2,1,0,4,3:T(2,128)(2,1)}, f32[2,2,512,8,64]{2,4,3,1,0:T(8,128)}, f32[2,2,512,8,64]{2,4,3,1,0:T(8,128)}, bf16[2,2...) while((s32[]{:T(128)}, ...), condition=%wide.region_22.23_spmd, body=%wide.region_20.22_spmd.sunk | while | flops 1368387584 | bytes 95015136 | solution.py:241
  427.5 9.4 %fusion.69 = bf16[1,512,2048]{2,1,0:T(8,128)(2,1)} fusion(bf16[16,134,512]{2,1,0:T(8,128)(2,1)} %all-to-all-done, bf16[16,1,134,2048]{3,2,0,1:T(8,128)(2,1)} %copy-done.57), kind=kOutput, calls=%fused_computation.94 | convolution fusion | flops 4497342464 | bytes 13074432 | tf_op jit(solution)/shard_map/sxcd,sxcf->xdf/dot_general | solution.py:181
  437.6 10.9 %fusion.72 = bf16[1,2048,512]{2,1,0:T(8,128)(2,1)} fusion(bf16[16,134,512]{2,1,0:T(8,128)(2,1)} %all-to-all-done.2, f32[16,134,2048]{2,1,0:T(8,128)S(1)} %copy-done.56, f32[2048]{0:T(1024)S(1)} %bitcast.315), kind=kOutput, calls=%fused_computation.95 | convolution fusion | flops 4541251584 | bytes 21864448 | tf_op jit(solution)/shard_map/sxcf,sxcd->xfd/dot_general | solution.py:172
  451.5 7.3 all-reduce.2
  464.7 23.1 %reduce-scatter.3.cloned.1.call-done = f32[4,256,512]{1,2,0:T(8,128)} async-done(((f32[4,512,512]{1,2,0:T(8,128)}), f32[4,256,512]{1,2,0:T(8,128)}) %reduce-scatter.3.cloned.1.call-update) | async-done | bytes 2097168 | tf_op jit(solution)/shard_map/reduce_scatter | solution.py:245
  493.1 51.3 %reduce-scatter.5.cloned.1.call-done = f32[4,256,512]{1,2,0:T(8,128)} async-done(((f32[4,512,512]{1,2,0:T(8,128)}), f32[4,256,512]{1,2,0:T(8,128)}) %reduce-scatter.5.cloned.1.call-update) | async-done | bytes 2097168 | tf_op jit(solution)/shard_map/reduce_scatter | solution.py:248
  549.9 5.4 fusion.103
  557.7 98.5 %all-reduce.9.cloned.1.call-done = (bf16[1,512,2048]{2,1,0:T(8,128)(2,1)}, bf16[1,2048,512]{2,1,0:T(8,128)(2,1)}) async-done(((bf16[1,512,2048]{2,1,0:T(8,128)(2,1)}, bf16[1,2048,512]{2,1,0:T(8,128)(2,1)}), (bf16[1,512,2048]{2,1,0:T(8,128)(2,1)}, bf16[1,2048,512]{2,1,0:T(8,128)(2,1)})) %all-reduce.9.cloned.1.call-update) | async-done | bytes 4194320 | tf_op jit(solution)/shard_map/psum | solution.py:197
  656.1 4.3 convert_element_type.174
  664.7 3.6 fusion.96
  668.3 40.5 %all-reduce = (f32[512]{0:T(512)}, f32[512]{0:T(512)}, f32[512,16]{0,1:T(8,128)}, f32[3]{0:T(128)S(1)}) all-reduce(f32[512]{0:T(512)S(1)} %get-tuple-element.193, f32[512]{0:T(512)S(1)} %copy-done.43, f32[512,16]{0,1:T(8,128)S(1)} %fusion.128, f32[3]{0:T(128)S(1)} %pad_maximum_fusion.3), channel_id=1, replica_groups=mesh['wide'=16,'narrow'=2] {'wide','narrow'}, use_global_device_ids=true, to_apply=%region_28.29 | all-reduce | flops 9219 | bytes 73752 | tf_op jit(solution)/shard_map/psum | solution.py:259
  709.3 3.1 fusion.95
  712.4 93.7 %all-reduce.7.cloned.1.call-done = (f32[512,1536]{1,0:T(8,128)}, f32[512,512]{1,0:T(8,128)}) async-done(((f32[512,1536]{1,0:T(8,128)}, f32[512,512]{1,0:T(8,128)}), (f32[512,1536]{1,0:T(8,128)}, f32[512,512]{1,0:T(8,128)})) %all-reduce.7.cloned.1.call-update) | async-done | bytes 4194320 | tf_op jit(solution)/shard_map/psum | solution.py:259
  806.1 3.9 copy.197
  (238 shorter events, 130.9 us)
Async XLA Ops:
  7.2 209.2 %copy-start = (bf16[1,2048,512]{2,1,0:T(8,128)(2,1)S(1)}, bf16[1,2048,512]{2,1,0:T(8,128)(2,1)}, u32[]{:S(2)}) copy-start(bf16[1,2048,512]{2,1,0:T(8,128)(2,1)} %param.27) | copy-start | bytes 6291460
  7.2 4.7 copy-start.10
  7.2 45.5 %all-gather.3.cloned.1.call-start = ((), (), s32[]{:S(2)}) async-start(), calls=%async_computation.6 | async-start | bytes 3145728 | tf_op jit(solution)/shard_map/all_gather | solution.py:69
  7.3 6.1 copy-start.53
  16.7 71.2 %all-gather.5.cloned.1.call-start = ((), (), s32[]{:S(2)}) async-start(), calls=%async_computation.7 | async-start | bytes 3145728 | tf_op jit(solution)/shard_map/all_gather | solution.py:68
  19.7 2.3 copy-start.44
  19.7 2.3 copy-start.45
  111.0 6.0 copy-start.32
  141.9 49.1 %all-to-all-start = ((bf16[16,134,512]{2,1,0:T(8,128)(2,1)}), bf16[16,134,512]{2,1,0:T(8,128)(2,1)}, u32[]{:S(2)}, u32[]{:S(2)}) async-start(bf16[16,134,512]{2,1,0:T(8,128)(2,1)} %reshape.368), calls=%async_computation | async-start | bytes 4456448 | tf_op jit(solution)/shard_map/all_to_all | solution.py:116
  154.2 6.1 copy-start.35
  181.0 22.2 %copy-start.46 = (bf16[1,2048]{1,0:T(2,128)(2,1)S(1)}, bf16[1,2048]{1,0:T(2,128)(2,1)}, u32[]{:S(2)}) copy-start(bf16[1,2048]{1,0:T(2,128)(2,1)} %param.26) | copy-start | bytes 12292
  181.0 22.2 %copy-start.50 = (bf16[1,512]{1,0:T(2,128)(2,1)S(1)}, bf16[1,512]{1,0:T(2,128)(2,1)}, u32[]{:S(2)}) copy-start(bf16[1,512]{1,0:T(2,128)(2,1)} %param.28) | copy-start | bytes 3076
  191.0 55.5 %all-to-all-start.2 = ((bf16[16,134,512]{2,1,0:T(8,128)(2,1)}), bf16[16,134,512]{2,1,0:T(8,128)(2,1)}, u32[]{:S(2)}, u32[]{:S(2)}) async-start(bf16[16,134,512]{2,1,0:T(8,128)(2,1)} %reshape.377), calls=%async_computation.2 | async-start | bytes 4456448 | tf_op jit(solution)/shard_map/all_to_all | solution.py:165
  203.1 55.7 %copy-start.47 = (f32[1,2048]{1,0:T(1,128)}, f32[1,2048]{1,0:T(1,128)S(1)}, u32[]{:S(2)}) copy-start(f32[1,2048]{1,0:T(1,128)S(1)} %add.177) | copy-start | bytes 24580
  210.2 6.1 copy-start.55
  246.5 55.7 %all-to-all-start.1 = ((bf16[16,134,512]{2,1,0:T(8,128)(2,1)}), bf16[16,134,512]{2,1,0:T(8,128)(2,1)}, u32[]{:S(2)}, u32[]{:S(2)}) async-start(bf16[16,134,512]{2,1,0:T(8,128)(2,1)} %fusion.75), calls=%async_computation.1 | async-start | bytes 4456448 | tf_op jit(solution)/shard_map/all_to_all | solution.py:129
  258.8 24.4 %copy-start.52 = (bf16[1,512,2048]{2,1,0:T(8,128)(2,1)S(1)}, bf16[1,512,2048]{2,1,0:T(8,128)(2,1)}, u32[]{:S(2)}) copy-start(bf16[1,512,2048]{2,1,0:T(8,128)(2,1)} %param.25) | copy-start | bytes 6291460
  279.7 3.5 copy-start.57
  289.6 24.7 %copy-start.14 = (bf16[4,256,512]{2,1,0:T(8,128)(2,1)S(1)}, bf16[4,256,512]{2,1,0:T(8,128)(2,1)}, u32[]{:S(2)}) copy-start(bf16[4,256,512]{2,1,0:T(8,128)(2,1)} %param.19) | copy-start | bytes 3145732
  302.2 55.2 %all-to-all-start.3 = ((bf16[16,134,512]{2,1,0:T(8,128)(2,1)}), bf16[16,134,512]{2,1,0:T(8,128)(2,1)}, u32[]{:S(2)}, u32[]{:S(2)}) async-start(bf16[16,134,512]{2,1,0:T(8,128)(2,1)} %fusion.98), calls=%async_computation.3 | async-start | bytes 4456448 | tf_op jit(solution)/shard_map/all_to_all | solution.py:189
  314.0 2.9 copy-start.40
  314.0 173.8 %reduce-scatter.3.cloned.1.call-start = ((), (), s32[]{:S(2)}) async-start(), calls=%async_computation.8 | async-start | bytes 6291456 | tf_op jit(solution)/shard_map/reduce_scatter | solution.py:245
  329.8 5.6 copy-start.16
  348.0 34.5 %copy-start.30 = (bf16[1024,16]{0,1:T(8,128)(2,1)}, bf16[1024,16]{0,1:T(8,128)(2,1)S(1)}, u32[]{:S(2)}) copy-start(bf16[1024,16]{0,1:T(8,128)(2,1)S(1)} %multiply_convert_fusion.7) | copy-start | bytes 98308
  369.3 5.5 copy-start.22
  374.8 7.7 copy-start.7
  384.5 4.3 copy-start.29
  391.6 4.7 copy-start.2
  391.6 4.7 copy-start.33
  426.9 117.5 %reduce-scatter.5.cloned.1.call-start = ((), (), s32[]{:S(2)}) async-start(), calls=%async_computation.9 | async-start | bytes 6291456 | tf_op jit(solution)/shard_map/reduce_scatter | solution.py:248
  427.4 9.4 %copy-start.48 = (f32[1,2048]{1,0:T(1,128)S(1)}, f32[1,2048]{1,0:T(1,128)}, u32[]{:S(2)}) copy-start(f32[1,2048]{1,0:T(1,128)} %copy-done.47) | copy-start | bytes 24580
  427.5 228.7 %all-reduce.9.cloned.1.call-start = ((), (), s32[]{:S(2)}) async-start(), calls=%async_computation.11 | async-start | bytes 8388608 | tf_op jit(solution)/shard_map/psum | solution.py:197
  427.5 10.1 %copy-start.56 = (f32[16,134,2048]{2,1,0:T(8,128)S(1)}, f32[16,134,2048]{2,1,0:T(8,128)}, u32[]{:S(2)}) copy-start(f32[16,134,2048]{2,1,0:T(8,128)} %copy-done.55) | copy-start | bytes 52690948
  448.5 11.5 %copy-start.20 = (bf16[2,2,256,8,64]{2,1,0,4,3:T(2,128)(2,1)S(1)}, bf16[2,2,256,8,64]{2,1,0,4,3:T(2,128)(2,1)}, u32[]{:S(2)}) copy-start(bf16[2,2,256,8,64]{2,1,0,4,3:T(2,128)(2,1)} %get-tuple-element.96) | copy-start | bytes 3145732
  448.5 13.3 %copy-start.5 = (f32[1024,512]{1,0:T(8,128)S(1)}, f32[1024,512]{1,0:T(8,128)}, u32[]{:S(2)}) copy-start(f32[1024,512]{1,0:T(8,128)} %copy-done.4) | copy-start | bytes 6291460
  448.5 357.6 %all-reduce.7.cloned.1.call-start = ((), (), s32[]{:S(2)}) async-start(), calls=%async_computation.10 | async-start | bytes 8388608 | tf_op jit(solution)/shard_map/psum | solution.py:259
  656.1 4.3 copy-start.21
  660.4 2.8 copy-start.11
  660.4 2.8 copy-start.25
  660.4 2.8 copy-start.26
  660.4 3.6 copy-start.28
  660.4 3.6 copy-start.37
  660.5 3.6 copy-start.39
  660.5 3.6 copy-start.42
  660.5 4.2 copy-start.54
  664.7 3.6 copy-start.43
  806.1 3.9 copy-start.24
  806.1 4.9 copy-start.1
  (25 other events, 36.3 us)
Sparse Core Ops, SparseCore 0:
  16.8 35.8 all-gather.2
  54.8 33.1 all-gather.4
  427.0 60.7 reduce-scatter.2
  490.1 54.2 reduce-scatter.4
  547.9 108.2 all-reduce.8
  663.2 142.7 all-reduce.6
where the time goes:
time: 823 us; the launch traced here: 818 us
  waiting for transfers between devices  381 us (46%)
  local copies, waits for them, and re-layouts  146 us (18%)
  matrix products  116 us (14%)
  other arithmetic  70 us (9%)
  blocking collectives  47.8 us (6%)
  starting transfers between devices  42.2 us (5%)
  between operations  15 us (2%)
    psum x1, waiting for transfers between devices, shards(): lax.psum(d_expert_in.astype(jnp.bfloat16), 'narrow').astype(jnp.float32)  98.5 us
    psum x1, waiting for transfers between devices, shards(): lax.psum((d_gain_one, d_qkv_weight, d_attn_weight, d_gain_two, d_router),...  93.7 us
    reduce_scatter x1, waiting for transfers between devices, shards(): lax.psum_scatter(value_terms.reshape(images, seq_len, width), 'narrow', s...  51.3 us
    psum x1, blocking collectives, shards(): lax.psum((d_gain_one, d_qkv_weight, d_attn_weight, d_gain_two, d_router),...  40.5 us
    all_gather x1, waiting for transfers between devices, shards(): lax.all_gather(keys_own, 'narrow', axis=1, tiled=True)  31.1 us
    all_gather x1, waiting for transfers between devices, shards(): lax.all_gather(values_own, 'narrow', axis=1, tiled=True)  27.6 us
    reduce_scatter x1, waiting for transfers between devices, shards(): lax.psum_scatter(key_terms.reshape(images, seq_len, width), 'narrow', sca...  23.1 us
    unnamed x110, local copies, waits for them, and re-layouts  23 us
  transfers between devices with their start and end apart: 10, of which 10 were waited for; matrix products, arithmetic and copies ran while one was open for 22% of the time, Pallas kernels for 0%

commit v1 on v0

v1 whole, which is shorter than its diff:
```python
import functools
import math

import jax
import jax.numpy as jnp
from jax import lax
from jax.experimental import pallas as pl
from jax.experimental.pallas import tpu as pltpu
from jax.sharding import PartitionSpec as P

HEADS = 8
TOP = 2


EPS = 1e-06
BF16 = jnp.bfloat16
F32 = jnp.float32
MIB = 1 << 20


def normalize(values):
    centre = jnp.mean(values, -1, keepdims=True)
    shifted = values - centre
    inverse = lax.rsqrt(jnp.mean(shifted * shifted, -1, keepdims=True) + EPS)
    return (shifted * inverse, inverse)


def norm_back(d_normed, normed, inverse):
    return inverse * (
        d_normed
        - jnp.mean(d_normed, -1, keepdims=True)
        - normed * jnp.mean(d_normed * normed, -1, keepdims=True)
    )


def dot(left, right, left_dim=1, right_dim=0):
    return lax.dot_general(
        left, right, (((left_dim,), (right_dim,)), ((), ())), preferred_element_type=F32
    )


def params(mib):
    return pltpu.CompilerParams(vmem_limit_bytes=mib * MIB)


def cost(flops, bytes_accessed, transcendentals=0):
    return pl.CostEstimate(
        flops=int(flops), bytes_accessed=int(bytes_accessed), transcendentals=int(transcendentals)
    )


def whole(shape):
    return pl.BlockSpec(shape, lambda *unused: (0,) * len(shape))


def hits(slots, places):
    first, second = slots
    return jnp.where((places == first) | (places == second), 1.0, 0.0).astype(BF16)


def put_rows(slots_ref, rows_ref, out_ref):
    step = out_ref.shape[0]
    places = lax.broadcasted_iota(jnp.int32, (step, rows_ref.shape[0]), 0) + pl.program_id(0) * step
    out_ref[...] = dot(hits((slots_ref[0:1, :], slots_ref[1:2, :]), places), rows_ref[...]).astype(
        BF16
    )


def dispatch_rows(slot_rows, rows, total, steps=8):
    tokens, width = rows.shape
    step = total // steps
    return pl.pallas_call(
        put_rows,
        grid=(steps,),
        in_specs=[whole(slot_rows.shape), whole(rows.shape)],
        out_specs=pl.BlockSpec((step, width), lambda i: (i, 0)),
        out_shape=jax.ShapeDtypeStruct((total, width), BF16),
        compiler_params=params(32),
        cost_estimate=cost(2 * total * tokens * width, 4 * total * width),
        name="dispatch_rows",
    )(slot_rows, rows)


def attend_kernel(
    flag_ref, own_ref, far_ref, gain_ref, wt_ref, own_out, far_out, proj_ref, total_ref, mixed
):
    del flag_ref
    rows, width = own_ref.shape[1], own_ref.shape[2]
    head_dim = width // HEADS
    scale = head_dim ** (-0.5)
    x_float = jnp.concatenate([own_ref[0], far_ref[0]], 0).astype(F32)
    normed, unused = normalize(x_float)
    normed = (normed * gain_ref[...]).astype(BF16)
    proj_ref[0] = dot(wt_ref[...], normed, 1, 1).astype(BF16)

    def head(h, carry):
        at = pl.multiple_of(h * head_dim, head_dim)
        query = proj_ref[0, pl.ds(at, head_dim), :]
        key = proj_ref[0, pl.ds(at + width, head_dim), :]
        value = proj_ref[0, pl.ds(at + 2 * width, head_dim), :]
        scores = dot(key, query, 0, 0) * scale
        top = jnp.max(scores, 0, keepdims=True)
        exponent = jnp.exp(scores - top)
        total = jnp.sum(exponent, 0, keepdims=True)
        out = dot(value, exponent.astype(BF16)) * (1.0 / total)
        mixed[pl.ds(at, head_dim), :] = out
        total_ref[0, pl.ds(h, 1), :] = top + jnp.log(total)
        return carry

    lax.fori_loop(0, HEADS, head, 0)
    heads_out = mixed[...].T.astype(BF16)
    own_out[0] = heads_out[:rows]
    far_out[0] = heads_out[rows:]


def attend(flag, inputs, far, gain, w_qkv_t):
    part, rows, width = far.shape
    seq_len = 2 * rows
    block = lambda *shape: pl.BlockSpec((1,) + shape, lambda i, flag_ref: (i,) + (0,) * len(shape))
    return pl.pallas_call(
        attend_kernel,
        grid_spec=pltpu.PrefetchScalarGridSpec(
            num_scalar_prefetch=1,
            grid=(part,),
            in_specs=[
                pl.BlockSpec((1, rows, width), lambda i, flag_ref: (i + flag_ref[0] * part, 0, 0)),
                block(rows, width),
                whole(gain.shape),
                whole(w_qkv_t.shape),
            ],
            out_specs=[
                block(rows, width),
                block(rows, width),
                block(3 * width, seq_len),
                block(HEADS, seq_len),
            ],
            scratch_shapes=[pltpu.VMEM((width, seq_len), F32)],
        ),
        out_shape=[
            jax.ShapeDtypeStruct((part, rows, width), BF16),
            jax.ShapeDtypeStruct((part, rows, width), BF16),
            jax.ShapeDtypeStruct((part, 3 * width, seq_len), BF16),
            jax.ShapeDtypeStruct((part, HEADS, seq_len), F32),
        ],
        compiler_params=params(40),
        cost_estimate=cost(part * 8e9, 8 * MIB, part * HEADS * seq_len**2),
        name="attend",
    )(flag, inputs, far, gain, w_qkv_t)


def attend_back_kernel(
    flag_ref,
    own_ref,
    far_ref,
    gain_ref,
    wt_ref,
    proj_ref,
    total_ref,
    d_own_ref,
    d_far_ref,
    own_out,
    far_out,
    weight_out,
    gain_out,
    d_proj,
    d_mixed,
    weight_sum,
):
    del flag_ref
    image, last = pl.program_id(0), pl.num_programs(0) - 1
    rows, width = own_ref.shape[1], own_ref.shape[2]
    head_dim = width // HEADS
    scale = head_dim ** (-0.5)
    d_mixed[...] = jnp.concatenate([d_own_ref[0], d_far_ref[0]], 0).astype(F32).T.astype(BF16)

    def head(h, carry):
        at = pl.multiple_of(h * head_dim, head_dim)
        query = proj_ref[0, pl.ds(at, head_dim), :]
        key = proj_ref[0, pl.ds(at + width, head_dim), :]
        value = proj_ref[0, pl.ds(at + 2 * width, head_dim), :]
        d_out = d_mixed[pl.ds(at, head_dim), :]
        weights = jnp.exp(dot(key, query, 0, 0) * scale - total_ref[0, pl.ds(h, 1), :])
        product = weights * dot(value, d_out, 0, 0)
        spread = jnp.sum(product, 0, keepdims=True)
        d_scores = (product - weights * spread).astype(BF16)
        d_proj[pl.ds(at, head_dim), :] = (dot(key, d_scores) * scale).astype(BF16)
        d_proj[pl.ds(at + width, head_dim), :] = (dot(query, d_scores, 1, 1) * scale).astype(BF16)
        d_proj[pl.ds(at + 2 * width, head_dim), :] = dot(d_out, weights.astype(BF16), 1, 1).astype(
            BF16
        )
        return carry

    lax.fori_loop(0, HEADS, head, 0)
    x_float = jnp.concatenate([own_ref[0], far_ref[0]], 0).astype(F32)
    normed, inverse = normalize(x_float)
    d_input = dot(d_proj[...], wt_ref[...], 0, 0)
    weight_term = dot(d_proj[...], (normed * gain_ref[...]).astype(BF16))
    gain_term = jnp.sum(d_input * normed, 0, keepdims=True)
    d_x = norm_back(d_input * gain_ref[...], normed, inverse).astype(BF16)
    own_out[0] = d_x[:rows]
    far_out[0] = d_x[rows:]

    @pl.when(image == 0)
    def start():
        weight_sum[...] = weight_term
        gain_out[...] = gain_term

    @pl.when(image != 0)
    def add():
        weight_sum[...] += weight_term
        gain_out[...] += gain_term

    @pl.when(image == last)
    def finish():
        weight_out[...] = weight_sum[...].T


def attend_back(flag, inputs, far, gain, w_qkv_t, proj, total, d_heads, d_far):
    part, rows, width = far.shape
    seq_len = 2 * rows
    block = lambda *shape: pl.BlockSpec((1,) + shape, lambda i, flag_ref: (i,) + (0,) * len(shape))
    return pl.pallas_call(
        attend_back_kernel,
        grid_spec=pltpu.PrefetchScalarGridSpec(
            num_scalar_prefetch=1,
            grid=(part,),
            in_specs=[
                pl.BlockSpec((1, rows, width), lambda i, flag_ref: (i + flag_ref[0] * part, 0, 0)),
                block(rows, width),
                whole(gain.shape),
                whole(w_qkv_t.shape),
                block(3 * width, seq_len),
                block(HEADS, seq_len),
                block(rows, width),
                block(rows, width),
            ],
            out_specs=[
                block(rows, width),
                block(rows, width),
                whole((width, 3 * width)),
                whole((1, width)),
            ],
            scratch_shapes=[
                pltpu.VMEM((3 * width, seq_len), BF16),
                pltpu.VMEM((width, seq_len), BF16),
                pltpu.VMEM((3 * width, width), F32),
            ],
        ),
        out_shape=[
            jax.ShapeDtypeStruct((part, rows, width), BF16),
            jax.ShapeDtypeStruct((part, rows, width), BF16),
            jax.ShapeDtypeStruct((width, 3 * width), F32),
            jax.ShapeDtypeStruct((1, width), F32),
        ],
        compiler_params=params(48),
        cost_estimate=cost(part * 16e9, 12 * MIB, part * HEADS * seq_len**2),
        name="attend_back",
    )(flag, inputs, far, gain, w_qkv_t, proj, total, d_heads, d_far)


def residual_kernel(
    flag_ref,
    own_ref,
    far_ref,
    x_ref,
    w_out_ref,
    gain_ref,
    slots_ref,
    heads_out,
    resid_out,
    normed_out,
    rows_out,
    moments_out,
):
    images, rows, width = x_ref.shape
    part = own_ref.shape[0]

    @pl.when(pl.program_id(0) == 0)
    def tokens():
        moments = [jnp.zeros((1, width), F32), jnp.zeros((1, width), F32)]
        for i in range(images):
            mine = (flag_ref[0] == 0) == (i < part)
            heads = jnp.where(mine, own_ref[i % part], far_ref[i % part])
            attn = dot(heads, w_out_ref[...])
            resid = x_ref[i].astype(F32) + attn
            normed, unused = normalize(resid)
            at = pl.ds(i * rows, rows)
            heads_out[at, :] = heads
            resid_out[at, :] = resid
            normed_out[at, :] = (normed * gain_ref[...]).astype(BF16)
            moments[0] += jnp.sum(resid * resid, 0, keepdims=True)
            moments[1] += jnp.sum(attn * attn, 0, keepdims=True)
        moments_out[...] = jnp.concatenate(moments, 0)

    put_rows(slots_ref, normed_out, rows_out)


def residual_rows(flag, own, far, inputs, w_attn_out, gain, slot_rows, total, steps=8):
    images, rows, width = inputs.shape
    tokens = images * rows
    step = total // steps
    return pl.pallas_call(
        residual_kernel,
        grid_spec=pltpu.PrefetchScalarGridSpec(
            num_scalar_prefetch=1,
            grid=(steps,),
            in_specs=[
                whole(own.shape),
                whole(far.shape),
                whole(inputs.shape),
                whole(w_attn_out.shape),
                whole(gain.shape),
                whole(slot_rows.shape),
            ],
            out_specs=[
                whole((tokens, width)),
                whole((tokens, width)),
                whole((tokens, width)),
                pl.BlockSpec((step, width), lambda i, flag_ref: (i, 0)),
                whole((2, width)),
            ],
        ),
        out_shape=[
            jax.ShapeDtypeStruct((tokens, width), BF16),
            jax.ShapeDtypeStruct((tokens, width), F32),
            jax.ShapeDtypeStruct((tokens, width), BF16),
            jax.ShapeDtypeStruct((total, width), BF16),
            jax.ShapeDtypeStruct((2, width), F32),
        ],
        compiler_params=params(40),
        cost_estimate=cost(2 * (total + width) * tokens * width, 10 * MIB),
        name="residual_rows",
    )(flag, own, far, inputs, w_attn_out, gain, slot_rows)


def expert_kernel(
    capacity,
    slots,
    rows_ref,
    up_ref,
    own_ref,
    router_ref,
    w_in_ref,
    b_in_ref,
    w_out_ref,
    b_out_ref,
    y_out,
    back_out,
    act_out,
    d_hidden_out,
    d_y_out,
    b_in_sum,
    b_out_sum,
):
    step, width = rows_ref.shape
    hidden_width = w_in_ref.shape[1]
    chunk = 512
    rows, up = rows_ref[...], up_ref[...]
    logits = dot(rows, router_ref[...])
    gate = jnp.exp(logits - jnp.max(logits, -1, keepdims=True))
    gate = jnp.sum(gate * own_ref[...], -1, keepdims=True) / jnp.sum(gate, -1, keepdims=True)
    up_float = up.astype(F32)
    d_y = (gate * up_float).astype(BF16)
    d_y_out[...] = d_y
    y = jnp.zeros((step, width), F32)
    back = jnp.zeros((step, width), F32)
    first = pl.program_id(0) == 0

    def accumulate(ref, at, value):
        ref[:, at] = jnp.where(first, 0.0, ref[:, at]) + jnp.sum(
            value.astype(F32), 0, keepdims=True
        )

    for c in range(hidden_width // chunk):
        at = slice(c * chunk, (c + 1) * chunk)
        hidden = dot(rows, w_in_ref[:, at]) + b_in_ref[:, at]
        square = hidden * hidden
        root = math.sqrt(2.0 / math.pi)
        slope = jnp.tanh(hidden * (root + (root * 0.044715) * square))
        half = 0.5 * (1.0 + slope)
        act = (hidden * half).astype(BF16)
        d_gelu = half + (0.5 * hidden) * (1.0 - slope * slope) * (
            root + (3.0 * root * 0.044715) * square
        )
        d_hidden = (dot(d_y, w_out_ref[at, :], 1, 1) * d_gelu).astype(BF16)
        act_out[:, at] = act
        d_hidden_out[:, at] = d_hidden
        y += dot(act, w_out_ref[at, :])
        back += dot(d_hidden, w_in_ref[:, at], 1, 1)
        accumulate(b_in_sum, at, d_hidden)
    accumulate(b_out_sum, slice(0, width), d_y)
    y = (y + b_out_ref[...]).astype(BF16).astype(F32)
    d_weight = jnp.sum(y * up_float, -1, keepdims=True)
    y_out[...] = (y * gate).astype(BF16)
    row = lax.broadcasted_iota(jnp.int32, (step, width), 0)
    lane = lax.broadcasted_iota(jnp.int32, (step, width), 1)
    for s in range(step // slots):
        line = jnp.sum(jnp.where(row - s * slots == lane, d_weight, 0.0), 0, keepdims=True)
        line = jnp.where(lane[:1] < capacity, line, 0.0)
        high = line.astype(BF16).astype(F32)
        back = jnp.where(row == s * slots + capacity, high, back)
        back = jnp.where(row == s * slots + capacity + 1, line - high, back)
    back_out[...] = back.astype(BF16)


def expert_rows(
    rows, up, own, w_router, w_in, b_in, w_out, b_out, capacity, slots, steps=8
):
    total, width = rows.shape
    hidden_width = w_in.shape[1]
    step = total // steps
    block = lambda size: pl.BlockSpec((step, size), lambda i: (i, 0))
    return pl.pallas_call(
        functools.partial(expert_kernel, capacity, slots),
        grid=(steps,),
        in_specs=[
            block(width),
            block(width),
            whole(own.shape),
            whole(w_router.shape),
            whole(w_in.shape),
            whole(b_in.shape),
            whole(w_out.shape),
            whole(b_out.shape),
        ],
        out_specs=[
            block(width),
            block(width),
            block(hidden_width),
            block(hidden_width),
            block(width),
            whole((1, hidden_width)),
            whole((1, width)),
        ],
        out_shape=[
            jax.ShapeDtypeStruct((total, width), BF16),
            jax.ShapeDtypeStruct((total, width), BF16),
            jax.ShapeDtypeStruct((total, hidden_width), BF16),
            jax.ShapeDtypeStruct((total, hidden_width), BF16),
            jax.ShapeDtypeStruct((total, width), BF16),
            jax.ShapeDtypeStruct((1, hidden_width), F32),
            jax.ShapeDtypeStruct((1, width), F32),
        ],
        compiler_params=params(48),
        cost_estimate=cost(8 * total * width * hidden_width, 32 * MIB, total * hidden_width),
        name="expert_rows",
    )(rows, up, own, w_router, w_in, b_in, w_out, b_out)


def weight_kernel(left_ref, right_ref, out_ref, turned):
    @pl.when(pl.program_id(0) == 0)
    def turn():
        turned[...] = left_ref[...].T

    out_ref[...] = dot(turned[...], right_ref[...]).astype(BF16)


def weight_grad(left, right, block=512):
    total, width = left.shape
    hidden_width = right.shape[1]
    return pl.pallas_call(
        weight_kernel,
        grid=(hidden_width // block,),
        in_specs=[whole(left.shape), pl.BlockSpec((total, block), lambda i: (0, i))],
        out_specs=pl.BlockSpec((width, block), lambda i: (0, i)),
        out_shape=jax.ShapeDtypeStruct((width, hidden_width), BF16),
        scratch_shapes=[pltpu.VMEM((width, total), BF16)],
        compiler_params=params(40),
        cost_estimate=cost(2 * total * width * hidden_width, 14 * MIB),
        name="weight_grad",
    )(left, right)


def turned_sum_kernel(own_ref, far_ref, out_ref):
    out_ref[...] = (own_ref[...].astype(F32) + far_ref[...].astype(F32)).T


def turned_sum(own, far, block=512):
    width, hidden_width = own.shape
    return pl.pallas_call(
        turned_sum_kernel,
        grid=(hidden_width // block,),
        in_specs=[pl.BlockSpec((width, block), lambda i: (0, i))] * 2,
        out_specs=pl.BlockSpec((block, width), lambda i: (i, 0)),
        out_shape=jax.ShapeDtypeStruct((hidden_width, width), F32),
        compiler_params=params(32),
        cost_estimate=cost(width * hidden_width, 8 * width * hidden_width),
        name="turned_sum",
    )(own, far)


def combine_kernel(slots_ref, y_ref, resid_ref, out_ref, moment_ref):
    step, total = out_ref.shape[0], y_ref.shape[0]
    places = lax.broadcasted_iota(jnp.int32, (step, total), 1)
    moe = dot(hits((slots_ref[:, 0:1], slots_ref[:, 1:2]), places), y_ref[...])
    out_ref[...] = (resid_ref[...] + moe).astype(BF16)
    moment = jnp.sum(moe * moe, 0, keepdims=True)
    moment_ref[...] = jnp.where(pl.program_id(0) == 0, 0.0, moment_ref[...]) + moment


def combine_rows(slot_columns, y, resid, step):
    tokens, width = resid.shape
    total = y.shape[0]
    block = lambda size: pl.BlockSpec((step, size), lambda i: (i, 0))
    return pl.pallas_call(
        combine_kernel,
        grid=(tokens // step,),
        in_specs=[block(TOP), whole(y.shape), block(width)],
        out_specs=[block(width), whole((1, width))],
        out_shape=[
            jax.ShapeDtypeStruct((tokens, width), BF16),
            jax.ShapeDtypeStruct((1, width), F32),
        ],
        compiler_params=params(40),
        cost_estimate=cost(2 * total * tokens * width, 8 * MIB),
        name="combine_rows",
    )(slot_columns, y, resid)


def token_back_kernel(
    capacity,
    slots,
    flag_ref,
    columns_ref,
    lines_ref,
    back_ref,
    resid_ref,
    normed_ref,
    heads_ref,
    up_ref,
    w_out_ref,
    router_ref,
    gain_ref,
    d_resid_out,
    d_heads_out,
    attn_sum,
    router_sum,
    gain_sum,
    d_weights,
):
    del flag_ref
    step, width = resid_ref.shape
    total = back_ref.shape[0]
    experts = router_ref.shape[0]
    first = pl.program_id(0) == 0

    @pl.when(first)
    def columns():
        row = lax.broadcasted_iota(jnp.int32, (slots, 256), 0)
        lane = lax.broadcasted_iota(jnp.int32, (slots, 256), 1)
        for e in range(experts):
            block = back_ref[e * slots : (e + 1) * slots, 0:256].astype(F32)
            line = jnp.sum(jnp.where(row >= capacity, block, 0.0), 0, keepdims=True)
            column = jnp.sum(jnp.where(row == lane, line, 0.0), -1, keepdims=True)
            d_weights[e * slots : (e + 1) * slots, :] = jnp.broadcast_to(column, (slots, step))

    def accumulate(ref, value):
        ref[...] = jnp.where(first, 0.0, ref[...]) + value

    line_slots = (lines_ref[0:1, :], lines_ref[1:2, :])
    d_gates = []
    for e in range(experts):
        places = lax.broadcasted_iota(jnp.int32, (slots, step), 0) + e * slots
        hit = (places == line_slots[0]) | (places == line_slots[1])
        d_gates.append(
            jnp.sum(
                jnp.where(hit, d_weights[e * slots : (e + 1) * slots, :], 0.0), 0, keepdims=True
            )
        )
    d_gates = jnp.concatenate(d_gates, 0)
    logits = dot(router_ref[...], normed_ref[...], 1, 1)
    gates = jnp.exp(logits - jnp.max(logits, 0, keepdims=True))
    gates = gates / jnp.sum(gates, 0, keepdims=True)
    d_logits = (gates * (d_gates - jnp.sum(gates * d_gates, 0, keepdims=True))).astype(BF16)
    places = lax.broadcasted_iota(jnp.int32, (step, total), 1)
    d_normed = dot(hits((columns_ref[:, 0:1], columns_ref[:, 1:2]), places), back_ref[...])
    d_normed += dot(d_logits, router_ref[...], 0, 0)
    normed, inverse = normalize(resid_ref[...])
    d_resid = up_ref[...].astype(F32) + norm_back(d_normed * gain_ref[...], normed, inverse)
    d_attn = d_resid.astype(BF16)
    d_resid_out[...] = d_resid
    d_heads_out[...] = dot(d_attn, w_out_ref[...], 1, 1).astype(BF16)
    accumulate(attn_sum, dot(heads_ref[...], d_attn, 0, 0))
    accumulate(router_sum, dot(d_logits, normed_ref[...]))
    accumulate(gain_sum, jnp.sum(d_normed * normed, 0, keepdims=True))


def token_back(
    flag,
    slot_columns,
    slot_rows,
    back,
    resid,
    normed,
    heads,
    up,
    w_attn_out,
    w_router_t,
    gain,
    capacity,
    slots,
    step,
    part,
):
    tokens, width = resid.shape
    total = back.shape[0]
    experts = w_router_t.shape[0]
    images = tokens // step
    block = lambda size: pl.BlockSpec((step, size), lambda i, flag_ref: (i, 0))
    return pl.pallas_call(
        functools.partial(token_back_kernel, capacity, slots),
        grid_spec=pltpu.PrefetchScalarGridSpec(
            num_scalar_prefetch=1,
            grid=(images,),
            in_specs=[
                block(TOP),
                pl.BlockSpec((TOP, step), lambda i, flag_ref: (0, i)),
                whole(back.shape),
                block(width),
                block(width),
                block(width),
                block(width),
                whole(w_attn_out.shape),
                whole(w_router_t.shape),
                whole(gain.shape),
            ],
            out_specs=[
                block(width),
                pl.BlockSpec(
                    (step, width),
                    lambda i, flag_ref: (lax.rem(i + flag_ref[0] * part, images), 0),
                ),
                whole((width, width)),
                whole((experts, width)),
                whole((1, width)),
            ],
            scratch_shapes=[pltpu.VMEM((total, step), F32)],
        ),
        out_shape=[
            jax.ShapeDtypeStruct((tokens, width), F32),
            jax.ShapeDtypeStruct((tokens, width), BF16),
            jax.ShapeDtypeStruct((width, width), F32),
            jax.ShapeDtypeStruct((experts, width), F32),
            jax.ShapeDtypeStruct((1, width), F32),
        ],
        compiler_params=params(48),
        cost_estimate=cost(2 * (total + 2 * width) * tokens * width, 14 * MIB),
        name="token_back",
    )(
        flag,
        slot_columns,
        slot_rows,
        back,
        resid,
        normed,
        heads,
        up,
        w_attn_out,
        w_router_t,
        gain,
    )


def grad_sum_kernel(flag_ref, resid_ref, own_ref, far_ref, out_ref):
    mine = (flag_ref[0] == 0) == (pl.program_id(0) < pl.num_programs(0) // 2)
    out_ref[...] = resid_ref[...] + jnp.where(mine, own_ref[0], far_ref[0]).astype(F32)


def grad_sum(flag, d_resid, own, far):
    part, rows, width = own.shape
    tokens = d_resid.shape[0]
    pick = pl.BlockSpec((1, rows, width), lambda i, flag_ref: (lax.rem(i, part), 0, 0))
    return pl.pallas_call(
        grad_sum_kernel,
        grid_spec=pltpu.PrefetchScalarGridSpec(
            num_scalar_prefetch=1,
            grid=(tokens // rows,),
            in_specs=[pl.BlockSpec((rows, width), lambda i, flag_ref: (i, 0)), pick, pick],
            out_specs=pl.BlockSpec((rows, width), lambda i, flag_ref: (i, 0)),
        ),
        out_shape=jax.ShapeDtypeStruct((tokens, width), F32),
        compiler_params=params(16),
        cost_estimate=cost(tokens * width, 6 * MIB),
        name="grad_sum",
    )(flag, d_resid, own, far)


def sum_steps():
    steps = []
    for axis in ("wide", "narrow"):
        bit = 1
        while bit < lax.axis_size(axis):
            steps.append((axis, bit))
            bit *= 2
    return steps


def swap(value, axis, bit):
    return lax.ppermute(value, axis, [(i, i ^ bit) for i in range(lax.axis_size(axis))])


def sum_all(value):
    steps = sum_steps()
    for axis, bit in steps:
        half = value.shape[0] // 2
        side = (lax.axis_index(axis) // bit) % 2
        keep = lax.dynamic_slice_in_dim(value, side * half, half, 0)
        send = lax.dynamic_slice_in_dim(value, (1 - side) * half, half, 0).astype(BF16)
        value = keep + swap(send, axis, bit).astype(F32)
    value = value.astype(BF16)
    for axis, bit in reversed(steps):
        side = (lax.axis_index(axis) // bit) % 2
        far = swap(value, axis, bit)
        value = jnp.where(
            side == 0, jnp.concatenate([value, far], 0), jnp.concatenate([far, value], 0)
        )
    return value.astype(F32)


def sum_small(value):
    for axis, bit in sum_steps():
        value = value + swap(value, axis, bit)
    return value


def gathered_attention(inputs, gain_one, w_qkv):
    images, rows_dev, width = inputs.shape
    tokens = images * rows_dev
    head_dim = width // HEADS
    scale = head_dim ** (-0.5)
    seq_len = rows_dev * lax.axis_size("narrow")
    group = math.gcd(images, max(1, 512 // rows_dev))
    blocks = images // group
    normed_one, inverse_one = normalize(inputs.astype(F32).reshape(tokens, width))
    input_one = (normed_one * gain_one).astype(BF16)
    projected = jnp.dot(input_one, w_qkv, preferred_element_type=F32).astype(BF16)
    queries = projected[:, :width].reshape(images, rows_dev, width)
    keys_own = projected[:, width : 2 * width].reshape(images, rows_dev, width)
    values_own = projected[:, 2 * width :].reshape(images, rows_dev, width)
    keys_all = lax.all_gather(keys_own, "narrow", axis=1, tiled=True)
    values_all = lax.all_gather(values_own, "narrow", axis=1, tiled=True)
    query_blocks = queries.reshape(blocks, group, rows_dev, HEADS, head_dim)
    key_blocks = keys_all.reshape(blocks, group, seq_len, HEADS, head_dim)
    value_blocks = values_all.reshape(blocks, group, seq_len, HEADS, head_dim)

    def attend_block(operands):
        query_b, key_b, value_b = operands
        scores = jnp.einsum("gqhd,gkhd->ghqk", query_b, key_b, preferred_element_type=F32) * scale
        top_score = jnp.max(scores, -1, keepdims=True)
        exponent = jnp.exp(scores - top_score)
        total = jnp.sum(exponent, -1, keepdims=True)
        weights = (exponent / total).astype(BF16)
        mixed = jnp.einsum("ghqk,gkhd->gqhd", weights, value_b, preferred_element_type=F32)
        return (mixed.astype(BF16), (top_score + jnp.log(total))[..., 0])

    heads_out, log_total = lax.map(attend_block, (query_blocks, key_blocks, value_blocks))

    def back_block(operands):
        query_b, key_b, value_b, total_b, d_head_b = operands
        scores = jnp.einsum("gqhd,gkhd->ghqk", query_b, key_b, preferred_element_type=F32) * scale
        weights = jnp.exp(scores - total_b[..., None])
        d_weights = jnp.einsum("gqhd,gkhd->ghqk", d_head_b, value_b, preferred_element_type=F32)
        spread = jnp.sum(weights * d_weights, -1, keepdims=True)
        d_scores = (weights * (d_weights - spread)).astype(BF16)
        d_query = jnp.einsum("ghqk,gkhd->gqhd", d_scores, key_b, preferred_element_type=F32) * scale
        d_key = jnp.einsum("ghqk,gqhd->gkhd", d_scores, query_b, preferred_element_type=F32) * scale
        d_value = jnp.einsum(
            "ghqk,gqhd->gkhd", weights.astype(BF16), d_head_b, preferred_element_type=F32
        )
        return (d_query.astype(BF16), d_key, d_value)

    def back(d_heads, d_resid):
        d_head_blocks = d_heads.reshape(blocks, group, rows_dev, HEADS, head_dim)
        d_queries, key_terms, value_terms = lax.map(
            back_block, (query_blocks, key_blocks, value_blocks, log_total, d_head_blocks)
        )
        d_keys, d_values = (
            lax.psum_scatter(
                terms.reshape(images, seq_len, width), "narrow", scatter_dimension=1, tiled=True
            )
            .astype(BF16)
            .reshape(tokens, width)
            for terms in (key_terms, value_terms)
        )
        d_projected = jnp.concatenate([d_queries.reshape(tokens, width), d_keys, d_values], 1)
        d_weight = jnp.dot(input_one.T, d_projected, preferred_element_type=F32)
        d_input = jnp.dot(d_projected, w_qkv.T, preferred_element_type=F32)
        d_gain = jnp.sum(d_input * normed_one, 0, keepdims=True)
        return (
            d_resid + norm_back(d_input * gain_one, normed_one, inverse_one),
            d_weight,
            d_gain,
        )

    return heads_out.reshape(images, rows_dev, width), back


def shards(
    inputs,
    cotangent,
    ln1_gain,
    w_qkv,
    w_attn_out,
    ln2_gain,
    w_router,
    expert_in,
    expert_in_bias,
    expert_out,
    expert_out_bias,
    route_ids,
    route_slots,
    route_dropped,
):
    images, rows_dev, width = inputs.shape
    tokens = images * rows_dev
    experts = w_router.shape[1]
    n_wide = lax.axis_size("wide")
    n_narrow = lax.axis_size("narrow")
    capacity = max(2, 42 * tokens // (20 * experts))
    slots = -(-(capacity + 2) // 8) * 8
    total = experts * slots
    gain_one = ln1_gain.astype(F32).reshape(1, width)
    gain_two = ln2_gain.astype(F32).reshape(1, width)
    paired = n_narrow == 2 and images % 2 == 0
    part = images // 2
    place = lax.axis_index("narrow") if paired else jnp.int32(0)
    flag = place.reshape(1)

    if paired:
        far_inputs = swap(
            lax.dynamic_slice_in_dim(inputs, (1 - place) * part, part, 0), "narrow", 1
        )

    slot_columns = jnp.where(
        route_dropped == 0, route_ids * slots + route_slots, -1
    ).reshape(tokens, TOP)
    slot_rows = slot_columns.T
    up = cotangent.reshape(tokens, width)

    def exchange(rows):
        return lax.all_to_all(
            rows.reshape(experts, slots, width), "wide", split_axis=0, concat_axis=0, tiled=True
        ).reshape(total, width)

    up_here = exchange(dispatch_rows(slot_rows, up, total))

    if paired:
        w_qkv_t = w_qkv.T
        heads_own, heads_far, proj, log_total = attend(
            flag, inputs, far_inputs, gain_one, w_qkv_t
        )
        heads_far = swap(heads_far, "narrow", 1)
    else:
        heads_own, attention_back = gathered_attention(inputs, gain_one, w_qkv)
        heads_own, heads_far = heads_own[:part], heads_own[part:]

    heads, resid, normed_two, rows, moments = residual_rows(
        flag, heads_own, heads_far, inputs, w_attn_out, gain_two, slot_rows, total
    )
    rows_here = exchange(rows)
    own = (jnp.arange(experts) == lax.axis_index("wide")).astype(F32).reshape(1, experts)
    w_in, w_out = expert_in[0], expert_out[0]
    y, back, act, d_hidden, d_y, b_in_sum, b_out_sum = expert_rows(
        rows_here,
        up_here,
        own,
        w_router,
        w_in,
        expert_in_bias.astype(F32),
        w_out,
        expert_out_bias.astype(F32),
        capacity,
        slots,
    )
    back = exchange(back)
    y = exchange(y)
    grad_out_t = weight_grad(d_y, act)
    grad_in = weight_grad(rows_here, d_hidden)
    biases = jnp.concatenate([b_in_sum, b_out_sum], 1)
    if n_narrow == 2:
        grad_expert_out = turned_sum(grad_out_t, swap(grad_out_t, "narrow", 1))
        grad_expert_in = grad_in.astype(F32) + swap(grad_in, "narrow", 1).astype(F32)
        biases = biases + swap(biases, "narrow", 1)
    else:
        grad_out_t, grad_in = lax.psum((grad_out_t, grad_in), "narrow")
        grad_expert_out = grad_out_t.astype(F32).T
        grad_expert_in = grad_in.astype(F32)
        biases = lax.psum(biases, "narrow")

    d_resid, d_heads, attn_term, router_term, gain_two_term = token_back(
        flag,
        slot_columns,
        slot_rows,
        back,
        resid,
        normed_two,
        heads,
        up,
        w_attn_out,
        w_router.T,
        gain_two,
        capacity,
        slots,
        rows_dev,
        part,
    )
    d_heads = d_heads.reshape(images, rows_dev, width)
    if paired:
        d_far = swap(d_heads[part:], "narrow", 1)
        d_own, d_far, qkv_term, gain_one_term = attend_back(
            flag, inputs, far_inputs, gain_one, w_qkv_t, proj, log_total, d_heads, d_far
        )
        input_grad = grad_sum(flag, d_resid, d_own, swap(d_far, "narrow", 1))
    else:
        input_grad, qkv_term, gain_one_term = attention_back(d_heads, d_resid)

    block_out, moe_moment = combine_rows(slot_columns, y, resid, rows_dev)
    small = jnp.concatenate([router_term, gain_one_term, gain_two_term, moments, moe_moment], 0)
    small = sum_small(small)
    grad_attn_out = sum_all(attn_term)
    grad_qkv = sum_all(qkv_term)
    moment_count = tokens * width * n_wide * n_narrow
    stats = jnp.sqrt(jnp.sum(small[experts + 2 : experts + 5], 1) / moment_count + EPS)
    return (
        block_out.reshape(images, rows_dev, width),
        input_grad.reshape(images, rows_dev, width),
        small[experts],
        grad_qkv,
        grad_attn_out,
        small[experts + 1],
        small[:experts].T,
        grad_expert_in[None],
        biases[:, : w_in.shape[1]],
        grad_expert_out[None],
        biases[:, w_in.shape[1] :],
        stats,
    )


def solution(mesh):
    return jax.shard_map(
        shards,
        mesh=mesh,
        in_specs=(
            P("wide", "narrow", None),
            P("wide", "narrow", None),
            P(),
            P(),
            P(),
            P(),
            P(),
            P("wide", None, None),
            P("wide", None),
            P("wide", None, None),
            P("wide", None),
            P("wide", "narrow", None),
            P("wide", "narrow", None),
            P("wide", "narrow", None),
        ),
        out_specs=(
            P("wide", "narrow", None),
            P("wide", "narrow", None),
            P(),
            P(),
            P(),
            P(),
            P(),
            P("wide", None, None),
            P("wide", None),
            P("wide", None, None),
            P("wide", None),
            P(),
        ),
        check_vma=False,
    )
```

time: 823 us -> 409 us (0.50)
  waiting for transfers between devices: 381 us -> 156 us
  Pallas kernels: 0 us -> 122 us
  matrix products: 116 us -> 0 us
  local copies, waits for them, and re-layouts: 146 us -> 39.6 us
  other arithmetic: 70 us -> 12.7 us
  blocking collectives: 47.8 us -> 0 us
  starting transfers between devices: 42.2 us -> 76.1 us
  between operations: 15 us -> 1.37 us
    psum x2 -> x0, waiting for transfers between devices: 192 us -> none  [the longest x1 98.5 us: shards(): lax.psum(d_expert_in.astype(jnp.bfloat16), 'narrow').astype(jnp.float32)]
    pallas_call x0 -> x11, Pallas kernels: none -> 122 us  [the longest x1 30.5 us: expert_rows(): pl.pallas_call(functools.partial(expert_kernel, capacity, slots), grid=(s...]
    dot_general x29 -> x0, matrix products: 116 us -> none  [the longest x1 20.9 us: shards(): jnp.einsum('sxcd,xfd->sxcf', d_produced, expert_out, preferred_element_ty...]
    reduce_scatter x2 -> x0, waiting for transfers between devices: 74.4 us -> none  [the longest x1 51.3 us: shards(): lax.psum_scatter(value_terms.reshape(images, seq_len, width), 'narrow', s...]
    ppermute x0 -> x32, waiting for transfers between devices: none -> 69.4 us  [swap(): lax.ppermute(value, axis, [(i, i ^ bit) for i in range(lax.axis_size(axis...]
    all_gather x2 -> x0, waiting for transfers between devices: 58.7 us -> none  [the longest x1 31.1 us: shards(): lax.all_gather(keys_own, 'narrow', axis=1, tiled=True)]
    psum x2 -> x0, blocking collectives: 47.8 us -> none  [the longest x1 40.5 us: shards(): lax.psum((d_gain_one, d_qkv_weight, d_attn_weight, d_gain_two, d_router),...]
    ppermute x0 -> x32, starting transfers between devices: none -> 39.3 us  [swap(): lax.ppermute(value, axis, [(i, i ^ bit) for i in range(lax.axis_size(axis...]
  transfers between devices with their start and end apart: 10 -> 36, of which waited for: 10 -> 14; matrix products, arithmetic and copies ran while one was open for 22% -> 4% of each run, Pallas kernels for 0% -> 18%
where the time goes in v1:
time: 409 us; the launch traced here: 408 us
  waiting for transfers between devices  156 us (38%)
  Pallas kernels  122 us (30%)
  starting transfers between devices  76.1 us (19%)
  local copies, waits for them, and re-layouts  39.6 us (10%)
  other arithmetic  12.7 us (3%)
    all_to_all x4, waiting for transfers between devices, exchange(): lax.all_to_all(rows.reshape(experts, slots, width), 'wide', split_axis=0,...  86.2 us
    ppermute x32, waiting for transfers between devices, swap(): lax.ppermute(value, axis, [(i, i ^ bit) for i in range(lax.axis_size(axis...  69.4 us
    ppermute x32, starting transfers between devices, swap(): lax.ppermute(value, axis, [(i, i ^ bit) for i in range(lax.axis_size(axis...  39.3 us
    all_to_all x4, starting transfers between devices, exchange(): lax.all_to_all(rows.reshape(experts, slots, width), 'wide', split_axis=0,...  36.8 us
    unnamed x89, local copies, waits for them, and re-layouts  32 us
    pallas_call x1, Pallas kernels, expert_rows(): pl.pallas_call(functools.partial(expert_kernel, capacity, slots), grid=(s...  30.5 us
    pallas_call x1, Pallas kernels, attend_back(): pl.pallas_call(attend_back_kernel, grid_spec=pltpu.PrefetchScalarGridSpec...  26.7 us
    pallas_call x2, Pallas kernels, weight_grad(): pl.pallas_call(weight_kernel, grid=(hidden_width // block,), in_specs=[wh...  15.5 us
  transfers between devices with their start and end apart: 36, of which 14 were waited for; matrix products, arithmetic and copies ran while one was open for 4% of the time, Pallas kernels for 18%

profile of v1, /device:TPU:0, one launch (start us, length us, event | category | flops | bytes accessed | tf_op | source)
XLA Modules:
  0.0 407.8 jit_solution(2626566243230215446)
XLA Ops:
  2.6 5.2 %dispatch_rows.1 = bf16[2176,512]{1,0:T(8,128)(2,1)} custom-call(s32[2,1024]{1,0:T(2,128)S(1)} %bitcast.37, bf16[1024,512]{1,0:T(8,128)(2,1)S(1)} %bitcast.49), custom_call_target="tpu_custom_call" | custom-call | flops 2281701376 | bytes 4456448 | tf_op jit(solution)/shard_map/dispatch_rows/pallas_call | solution.py:72
  7.8 7.5 %all-to-all-start.1 = ((bf16[16,136,512]{2,1,0:T(8,128)(2,1)}), bf16[16,136,512]{2,1,0:T(8,128)(2,1)}, u32[]{:S(2)}, u32[]{:S(2)}) async-start(bf16[16,136,512]{2,1,0:T(8,128)(2,1)} %bitcast.10), calls=%async_computation.1 | async-start | bytes 4456448 | tf_op jit(solution)/shard_map/all_to_all | solution.py:841
  16.2 1.5 collective-permute-start
  17.7 1.7 copy.27
  19.5 11.1 %collective-permute-done.far_ref = bf16[2,256,512]{2,1,0:T(8,128)(2,1)S(1)} collective-permute-done((bf16[2,256,512]{2,1,0:T(8,128)(2,1)}, bf16[2,256,512]{2,1,0:T(8,128)(2,1)S(1)}, u32[]{:S(2)}, u32[]{:S(2)}) %collective-permute-start) | collective-permute-done | bytes 524320 | tf_op jit(solution)/shard_map/ppermute | solution.py:699
  30.6 14.2 %attend.1 = (bf16[2,256,512]{2,1,0:T(8,128)(2,1)S(1)}, bf16[2,256,512]{2,1,0:T(8,128)(2,1)S(1)}, bf16[2,1536,512]{2,1,0:T(8,128)(2,1)S(1)}, f32[2,8,512]{2,1,0:T(8,128)S(1)}) custom-call(s32[1]{0:T(128)} %bitcast.1.flag_ref, bf16[4,256,512]{2,1,0:T(8,128)(2,1)S(1)} %copy-done.12, bf16[2,256,512]{2,1,0:T(8,128)(2,1)S(1)} %collective-permute-done.far_ref, ...), custom_call_target="tpu_custom_call" | custom-call | flops 16000000000 | bytes 8388608 | tf_op jit(solution)/shard_map/attend/pallas_call | solution.py:120
  44.8 1.7 copy-done.33
  48.0 11.9 %collective-permute-done.1.far_ref = bf16[2,256,512]{2,1,0:T(8,128)(2,1)S(1)} collective-permute-done((bf16[2,256,512]{2,1,0:T(8,128)(2,1)S(1)}, bf16[2,256,512]{2,1,0:T(8,128)(2,1)S(1)}, u32[]{:S(2)}, u32[]{:S(2)}) %collective-permute-start.1) | collective-permute-done | bytes 524320 | tf_op jit(solution)/shard_map/ppermute | solution.py:699
  59.9 5.2 %residual_rows.1 = (bf16[1024,512]{1,0:T(8,128)(2,1)S(1)}, f32[1024,512]{1,0:T(8,128)S(1)}, bf16[1024,512]{1,0:T(8,128)(2,1)S(1)}, bf16[2176,512]{1,0:T(8,128)(2,1)S(1)}, f32[2,512]{1,0:T(2,128)S(1)}) custom-call(s32[1]{0:T(128)} %bitcast.1.flag_ref, bf16[2,256,512]{2,1,0:T(8,128)(2,1)S(1)} %get-tuple-element.39.own_ref, ...), custom_call_target="tpu_custom_call" | custom-call | flops 2818572288 | bytes 10485760 | tf_op jit(solution)/shard_map/residual_rows/pallas_call | solution.py:302
  69.7 5.6 %all-to-all-start = ((bf16[16,136,512]{2,1,0:T(8,128)(2,1)}), bf16[16,136,512]{2,1,0:T(8,128)(2,1)S(1)}, u32[]{:S(2)}, u32[]{:S(2)}) async-start(bf16[16,136,512]{2,1,0:T(8,128)(2,1)} %bitcast.33), calls=%async_computation | async-start | bytes 4456448 | tf_op jit(solution)/shard_map/all_to_all | solution.py:841
  75.5 43.2 %all-to-all-done = bf16[16,136,512]{2,1,0:T(8,128)(2,1)S(1)} async-done(((bf16[16,136,512]{2,1,0:T(8,128)(2,1)}), bf16[16,136,512]{2,1,0:T(8,128)(2,1)S(1)}, u32[]{:S(2)}, u32[]{:S(2)}) %all-to-all-start) | async-done | bytes 2228256 | tf_op jit(solution)/shard_map/all_to_all | solution.py:841
  120.0 1.6 copy-done.15
  121.6 1.6 copy-done.16
  123.2 30.5 %expert_rows.1 = (bf16[2176,512]{1,0:T(8,128)(2,1)}, bf16[2176,512]{1,0:T(8,128)(2,1)}, bf16[2176,2048]{1,0:T(8,128)(2,1)}, bf16[2176,2048]{1,0:T(8,128)(2,1)}, ...) custom-call(bf16[2176,512]{1,0:T(8,128)(2,1)} %bitcast.30, ...), custom_call_target="tpu_custom_call" | custom-call | flops 18253611008 | bytes 33554432 | tf_op jit(solution)/shard_map/expert_rows/pallas_call | solution.py:413
  153.7 11.9 %all-to-all-start.3 = ((bf16[16,136,512]{2,1,0:T(8,128)(2,1)}), bf16[16,136,512]{2,1,0:T(8,128)(2,1)}, u32[]{:S(2)}, u32[]{:S(2)}) async-start(bf16[16,136,512]{2,1,0:T(8,128)(2,1)} %bitcast.52), calls=%async_computation.3 | async-start | bytes 4456448 | tf_op jit(solution)/shard_map/all_to_all | solution.py:841
  166.1 43.0 %all-to-all-done.3 = bf16[16,136,512]{2,1,0:T(8,128)(2,1)} async-done(((bf16[16,136,512]{2,1,0:T(8,128)(2,1)}), bf16[16,136,512]{2,1,0:T(8,128)(2,1)}, u32[]{:S(2)}, u32[]{:S(2)}) %all-to-all-start.3) | async-done | bytes 2228256 | tf_op jit(solution)/shard_map/all_to_all | solution.py:841
  211.6 14.0 %token_back.1 = (f32[1024,512]{1,0:T(8,128)}, bf16[1024,512]{1,0:T(8,128)(2,1)S(1)}, f32[512,512]{1,0:T(8,128)S(1)}, f32[16,512]{1,0:T(8,128)S(1)}, f32[1,512]{1,0:T(1,128)S(1)}) custom-call(s32[1]{0:T(128)} %bitcast.1.flag_ref, s32[1024,2]{1,0:T(8,128)S(1)} %copy.29.slots_ref.columns_ref, s32[2,1024]{1,0:T(2,128)S(1)} %bitcast.40, ...), custom_call_target="tpu_custom_call" | custom-call | flops 3355443200 | bytes 14680064 | tf_op jit(solution)/shard_map/token_back/pallas_call | solution.py:610
  228.0 3.5 copy-done.25
  231.5 7.8 %weight_grad.3.own_ref = bf16[512,2048]{1,0:T(8,128)(2,1)} custom-call(bf16[2176,512]{1,0:T(8,128)(2,1)S(1)} %copy-done.26, bf16[2176,2048]{1,0:T(8,128)(2,1)S(1)} %copy-done.25), custom_call_target="tpu_custom_call" | custom-call | flops 4563402752 | bytes 14680064 | tf_op jit(solution)/shard_map/weight_grad/pallas_call | solution.py:461
  241.3 11.7 %all-to-all-start.2 = ((bf16[16,136,512]{2,1,0:T(8,128)(2,1)}), bf16[16,136,512]{2,1,0:T(8,128)(2,1)S(1)}, u32[]{:S(2)}, u32[]{:S(2)}) async-start(bf16[16,136,512]{2,1,0:T(8,128)(2,1)} %bitcast.51), calls=%async_computation.2 | async-start | bytes 4456448 | tf_op jit(solution)/shard_map/all_to_all | solution.py:841
  259.1 26.7 %attend_back.1 = (bf16[2,256,512]{2,1,0:T(8,128)(2,1)S(1)}, bf16[2,256,512]{2,1,0:T(8,128)(2,1)S(1)}, f32[512,1536]{1,0:T(8,128)}, f32[1,512]{1,0:T(1,128)S(1)}) custom-call(s32[1]{0:T(128)} %bitcast.1.flag_ref, bf16[4,256,512]{2,1,0:T(8,128)(2,1)S(1)} %copy-done.13, bf16[2,256,512]{2,1,0:T(8,128)(2,1)S(1)} %copy-done.21, f32[1,512]{1,0:T(1,128)S(1)} %bitcast.43, ...), custom_call_target="tpu_custom_call" | custom-call | flops 32000000000 | bytes 12582912 | tf_op jit(solution)/shard_map/attend_back/pallas_call | solution.py:222
  289.1 3.5 copy-done.24
  292.6 7.7 %weight_grad.2 = bf16[512,2048]{1,0:T(8,128)(2,1)} custom-call(bf16[2176,512]{1,0:T(8,128)(2,1)S(1)} %bitcast.31, bf16[2176,2048]{1,0:T(8,128)(2,1)S(1)} %copy-done.24), custom_call_target="tpu_custom_call" | custom-call | flops 4563402752 | bytes 14680064 | tf_op jit(solution)/shard_map/weight_grad/pallas_call | solution.py:461
  301.0 2.0 collective-permute-start.20
  304.9 1.6 copy-done.28
  306.5 4.1 %combine_rows.1 = (bf16[1024,512]{1,0:T(8,128)(2,1)}, f32[1,512]{1,0:T(1,128)S(1)}) custom-call(s32[1024,2]{1,0:T(8,128)S(1)} %copy-done.7, bf16[2176,512]{1,0:T(8,128)(2,1)S(1)} %bitcast.32, f32[1024,512]{1,0:T(8,128)S(1)} %copy-done.28), custom_call_target="tpu_custom_call" | custom-call | flops 2281701376 | bytes 8388608 | tf_op jit(solution)/shard_map/combine_rows/pallas_call | solution.py:505
  311.6 1.6 collective-permute-start.21
  313.2 2.1 collective-permute-done.10
  316.5 1.5 collective-permute-start.11
  318.0 4.2 %collective-permute-done.11 = bf16[64,1536]{1,0:T(8,128)(2,1)S(1)} collective-permute-done((bf16[64,1536]{1,0:T(8,128)(2,1)S(1)}, bf16[64,1536]{1,0:T(8,128)(2,1)S(1)}, u32[]{:S(2)}, u32[]{:S(2)}) %collective-permute-start.11) | collective-permute-done | bytes 196640 | tf_op jit(solution)/shard_map/ppermute | solution.py:699
  322.3 2.4 collective-permute-start.12
  325.3 3.9 collective-permute-done.12
  329.3 1.6 collective-permute-start.13
  330.9 18.7 %collective-permute-done.13 = bf16[16,1536]{1,0:T(8,128)(2,1)S(1)} collective-permute-done((bf16[16,1536]{1,0:T(8,128)(2,1)S(1)}, bf16[16,1536]{1,0:T(8,128)(2,1)S(1)}, u32[]{:S(2)}, u32[]{:S(2)}) %collective-permute-start.13) | collective-permute-done | bytes 49184 | tf_op jit(solution)/shard_map/ppermute | solution.py:699
  351.7 2.0 collective-permute-done.14
  353.9 2.5 collective-permute-start.15
  356.4 1.6 collective-permute-start.24
  358.0 4.0 collective-permute-done.15
  362.0 1.6 collective-permute-start.5
  364.3 3.4 collective-permute-start.25
  369.7 4.1 collective-permute-start.26
  375.2 5.1 %add_bitcast_fusion = f32[1,512,2048]{2,1,0:T(8,128)} fusion(bf16[512,2048]{1,0:T(8,128)(2,1)} %collective-permute-done.29, bf16[512,2048]{1,0:T(8,128)(2,1)} %weight_grad.2), kind=kLoop, calls=%fused_computation | loop fusion | flops 3145728 | bytes 8388608 | tf_op jit(solution)/shard_map/broadcast_in_dim | solution.py:932
  380.3 5.2 %turned_sum.1 = f32[2048,512]{1,0:T(8,128)} custom-call(bf16[512,2048]{1,0:T(8,128)(2,1)} %weight_grad.3.own_ref, bf16[512,2048]{1,0:T(8,128)(2,1)} %collective-permute-done.31.far_ref), custom_call_target="tpu_custom_call" | custom-call | flops 1048576 | bytes 8388608 | tf_op jit(solution)/shard_map/turned_sum/pallas_call | solution.py:480
  385.6 2.1 collective-permute-start.8
  387.7 1.5 collective-permute-start.27
  389.2 9.7 %collective-permute-done.8 = f32[21,512]{1,0:T(8,128)S(1)} collective-permute-done((f32[21,512]{1,0:T(8,128)S(1)}, f32[21,512]{1,0:T(8,128)S(1)}, u32[]{:S(2)}, u32[]{:S(2)}) %collective-permute-start.8) | collective-permute-done | bytes 43040 | tf_op jit(solution)/shard_map/ppermute | solution.py:699
  403.5 1.9 grad_sum.1
  405.5 2.3 fusion
  (178 shorter events, 43.3 us)
Async XLA Ops:
  7.8 61.9 %all-to-all-start.1 = ((bf16[16,136,512]{2,1,0:T(8,128)(2,1)}), bf16[16,136,512]{2,1,0:T(8,128)(2,1)}, u32[]{:S(2)}, u32[]{:S(2)}) async-start(bf16[16,136,512]{2,1,0:T(8,128)(2,1)} %bitcast.10), calls=%async_computation.1 | async-start | bytes 4456448 | tf_op jit(solution)/shard_map/all_to_all | solution.py:841
  16.2 14.4 %collective-permute-start = (bf16[2,256,512]{2,1,0:T(8,128)(2,1)}, bf16[2,256,512]{2,1,0:T(8,128)(2,1)S(1)}, u32[]{:S(2)}, u32[]{:S(2)}) collective-permute-start(bf16[2,256,512]{2,1,0:T(8,128)(2,1)} %constant_dynamic-slice_fusion), channel_id=1, source_target_pairs={{0,1},{1,0},{2,3},{3,2},{4,5},{5,4},{6,7},{7,6},{8,9},{9,8},{10,11... | collective-permute-start | bytes 1572872 | tf_op jit(solution)/shard_map/ppermute | solution.py:699
  19.4 25.3 %copy-start.4 = (bf16[512,1536]{0,1:T(8,128)(2,1)}, bf16[512,1536]{0,1:T(8,128)(2,1)S(1)}, u32[]{:S(2)}) copy-start(bf16[512,1536]{0,1:T(8,128)(2,1)S(1)} %copy.27) | copy-start | bytes 4718596
  30.6 14.2 %copy-start.20 = (bf16[2,256,512]{2,1,0:T(8,128)(2,1)}, bf16[2,256,512]{2,1,0:T(8,128)(2,1)S(1)}, u32[]{:S(2)}) copy-start(bf16[2,256,512]{2,1,0:T(8,128)(2,1)S(1)} %collective-permute-done.far_ref) | copy-start | bytes 1572868
  30.6 17.4 %copy-start.42 = (bf16[512]{0:T(512)(128)(2,1)S(1)}, bf16[512]{0:T(512)(128)(2,1)}, u32[]{:S(2)}) copy-start(bf16[512]{0:T(512)(128)(2,1)} %param.19) | copy-start | bytes 3076
  30.6 29.3 %copy-start.18 = (bf16[512,512]{1,0:T(8,128)(2,1)S(1)}, bf16[512,512]{1,0:T(8,128)(2,1)}, u32[]{:S(2)}) copy-start(bf16[512,512]{1,0:T(8,128)(2,1)} %w_out_ref.3) | copy-start | bytes 1572868
  46.4 13.5 %collective-permute-start.1 = (bf16[2,256,512]{2,1,0:T(8,128)(2,1)S(1)}, bf16[2,256,512]{2,1,0:T(8,128)(2,1)S(1)}, u32[]{:S(2)}, u32[]{:S(2)}) collective-permute-start(bf16[2,256,512]{2,1,0:T(8,128)(2,1)S(1)} %get-tuple-element.40), channel_id=1, source_target_pairs={{0,1},{1,0},{2,3},{3,2},{4,5},{5,4},{6,7},{7,6},{8,9},{9,8},{10,11... | collective-permute-start | bytes 1572872 | tf_op jit(solution)/shard_map/ppermute | solution.py:699
  69.7 49.0 %all-to-all-start = ((bf16[16,136,512]{2,1,0:T(8,128)(2,1)}), bf16[16,136,512]{2,1,0:T(8,128)(2,1)S(1)}, u32[]{:S(2)}, u32[]{:S(2)}) async-start(bf16[16,136,512]{2,1,0:T(8,128)(2,1)} %bitcast.33), calls=%async_computation | async-start | bytes 4456448 | tf_op jit(solution)/shard_map/all_to_all | solution.py:841
  153.7 55.4 %copy-start.19 = (bf16[512,512]{1,0:T(8,128)(2,1)S(1)}, bf16[512,512]{1,0:T(8,128)(2,1)}, u32[]{:S(2)}) copy-start(bf16[512,512]{1,0:T(8,128)(2,1)} %w_out_ref.3) | copy-start | bytes 1572868
  153.7 55.4 %all-to-all-start.3 = ((bf16[16,136,512]{2,1,0:T(8,128)(2,1)}), bf16[16,136,512]{2,1,0:T(8,128)(2,1)}, u32[]{:S(2)}, u32[]{:S(2)}) async-start(bf16[16,136,512]{2,1,0:T(8,128)(2,1)} %bitcast.52), calls=%async_computation.3 | async-start | bytes 4456448 | tf_op jit(solution)/shard_map/all_to_all | solution.py:841
  166.0 59.5 %copy-start.6 = (s32[1024,2]{1,0:T(8,128)}, s32[1024,2]{1,0:T(8,128)S(1)}, u32[]{:S(2)}) copy-start(s32[1024,2]{1,0:T(8,128)S(1)} %copy.29.slots_ref.columns_ref) | copy-start | bytes 24580
  211.6 16.4 %copy-start.26 = (bf16[2176,512]{1,0:T(8,128)(2,1)S(1)}, bf16[2176,512]{1,0:T(8,128)(2,1)}, u32[]{:S(2)}) copy-start(bf16[2176,512]{1,0:T(8,128)(2,1)} %get-tuple-element.64.left_ref) | copy-start | bytes 6684676
  225.5 13.7 %copy-start.10 = (bf16[1024,512]{1,0:T(8,128)(2,1)}, bf16[1024,512]{1,0:T(8,128)(2,1)S(1)}, u32[]{:S(2)}) copy-start(bf16[1024,512]{1,0:T(8,128)(2,1)S(1)} %get-tuple-element.51) | copy-start | bytes 3145732
  226.4 27.8 %collective-permute-start.2 = (bf16[2,256,512]{2,1,0:T(8,128)(2,1)}, bf16[2,256,512]{2,1,0:T(8,128)(2,1)}, u32[]{:S(2)}, u32[]{:S(2)}) collective-permute-start(bf16[2,256,512]{2,1,0:T(8,128)(2,1)} %bitcast.21), channel_id=1, source_target_pairs={{0,1},{1,0},{2,3},{3,2},{4,5},{5,4},{6,7},{7,6},{8,9},{9,8},{10,11... | collective-permute-start | bytes 1572872 | tf_op jit(solution)/shard_map/ppermute | solution.py:699
  239.3 141.0 %collective-permute-start.31 = (bf16[512,2048]{1,0:T(8,128)(2,1)}, bf16[512,2048]{1,0:T(8,128)(2,1)}, u32[]{:S(2)}, u32[]{:S(2)}) collective-permute-start(bf16[512,2048]{1,0:T(8,128)(2,1)} %weight_grad.3.own_ref), channel_id=1, source_target_pairs={{0,1},{1,0},{2,3},{3,2},{4,5},{5,4},{6,7},{7,6},{8,9},{9,8},{10,11... | collective-permute-start | bytes 6291464 | tf_op jit(solution)/shard_map/ppermute | solution.py:699
  239.8 124.5 %collective-permute-start.30 = (f32[1,2560]{1,0:T(1,128)S(1)}, f32[1,2560]{1,0:T(1,128)S(1)}, u32[]{:S(2)}, u32[]{:S(2)}) collective-permute-start(f32[1,2560]{1,0:T(1,128)S(1)} %constant_dynamic-update-slice_fusion), channel_id=1, source_target_pairs={{0,1},{1,0},{2,3},{3,2},{4,5},{5,4},{6,7},{7,6},{8,9},{9,8},{10,11... | collective-permute-start | bytes 30728 | tf_op jit(solution)/shard_map/ppermute | solution.py:699
  241.3 63.6 %all-to-all-start.2 = ((bf16[16,136,512]{2,1,0:T(8,128)(2,1)}), bf16[16,136,512]{2,1,0:T(8,128)(2,1)S(1)}, u32[]{:S(2)}, u32[]{:S(2)}) async-start(bf16[16,136,512]{2,1,0:T(8,128)(2,1)} %bitcast.51), calls=%async_computation.2 | async-start | bytes 4456448 | tf_op jit(solution)/shard_map/all_to_all | solution.py:841
  253.8 47.0 %collective-permute-start.19 = (bf16[256,512]{1,0:T(8,128)(2,1)}, bf16[256,512]{1,0:T(8,128)(2,1)S(1)}, u32[]{:S(2)}, u32[]{:S(2)}) collective-permute-start(bf16[256,512]{1,0:T(8,128)(2,1)} %dynamic-slice_convert_fusion.2), channel_id=1, source_target_pairs={{0,2},{2,0},{4,6},{6,4},{8,10},{10,8},{12,14},{14,12},{16,18},{18,... | collective-permute-start | bytes 786440 | tf_op jit(solution)/shard_map/ppermute | solution.py:699
  259.1 30.0 %copy-start.1 = (bf16[16,136,512]{2,1,0:T(8,128)(2,1)S(1)}, bf16[16,136,512]{2,1,0:T(8,128)(2,1)}, u32[]{:S(2)}) copy-start(bf16[16,136,512]{2,1,0:T(8,128)(2,1)} %copy-done) | copy-start | bytes 6684676
  288.9 14.1 %collective-permute-start.9 = (bf16[256,1536]{1,0:T(8,128)(2,1)S(1)}, bf16[256,1536]{1,0:T(8,128)(2,1)S(1)}, u32[]{:S(2)}, u32[]{:S(2)}) collective-permute-start(bf16[256,1536]{1,0:T(8,128)(2,1)S(1)} %dynamic-slice_convert_fusion), channel_id=1, source_target_pairs={{0,2},{2,0},{4,6},{6,4},{8,10},{10,8},{12,14},{14,12},{16,18},{18,... | collective-permute-start | bytes 2359304 | tf_op jit(solution)/shard_map/ppermute | solution.py:699
  292.6 10.3 %copy-start.36 = (f32[512,1536]{1,0:T(8,128)S(1)}, f32[512,1536]{1,0:T(8,128)}, u32[]{:S(2)}) copy-start(f32[512,1536]{1,0:T(8,128)} %get-tuple-element.59) | copy-start | bytes 9437188
  300.3 74.9 %collective-permute-start.29 = (bf16[512,2048]{1,0:T(8,128)(2,1)}, bf16[512,2048]{1,0:T(8,128)(2,1)}, u32[]{:S(2)}, u32[]{:S(2)}) collective-permute-start(bf16[512,2048]{1,0:T(8,128)(2,1)} %weight_grad.2), channel_id=1, source_target_pairs={{0,1},{1,0},{2,3},{3,2},{4,5},{5,4},{6,7},{7,6},{8,9},{9,8},{10,11... | collective-permute-start | bytes 6291464 | tf_op jit(solution)/shard_map/ppermute | solution.py:699
  301.0 9.7 %collective-permute-start.20 = (bf16[128,512]{1,0:T(8,128)(2,1)S(1)}, bf16[128,512]{1,0:T(8,128)(2,1)}, u32[]{:S(2)}, u32[]{:S(2)}) collective-permute-start(bf16[128,512]{1,0:T(8,128)(2,1)S(1)} %dynamic-slice_convert_fusion.4), channel_id=1, source_target_pairs={{0,4},{2,6},{4,0},{6,2},{8,12},{10,14},{12,8},{14,10},{16,20},{18,... | collective-permute-start | bytes 393224 | tf_op jit(solution)/shard_map/ppermute | solution.py:699
  304.4 10.9 %collective-permute-start.10 = (bf16[128,1536]{1,0:T(8,128)(2,1)}, bf16[128,1536]{1,0:T(8,128)(2,1)}, u32[]{:S(2)}, u32[]{:S(2)}) collective-permute-start(bf16[128,1536]{1,0:T(8,128)(2,1)} %dynamic-slice_convert_fusion.1), channel_id=1, source_target_pairs={{0,4},{2,6},{4,0},{6,2},{8,12},{10,14},{12,8},{14,10},{16,20},{18,... | collective-permute-start | bytes 1179656 | tf_op jit(solution)/shard_map/ppermute | solution.py:699
  311.6 6.4 %collective-permute-start.21 = (bf16[64,512]{1,0:T(8,128)(2,1)S(1)}, bf16[64,512]{1,0:T(8,128)(2,1)S(1)}, u32[]{:S(2)}, u32[]{:S(2)}) collective-permute-start(bf16[64,512]{1,0:T(8,128)(2,1)S(1)} %dynamic-slice_convert_fusion.6), channel_id=1, source_target_pairs={{0,8},{2,10},{4,12},{6,14},{8,0},{10,2},{12,4},{14,6},{16,24},{18,... | collective-permute-start | bytes 196616 | tf_op jit(solution)/shard_map/ppermute | solution.py:699
  316.5 5.7 %collective-permute-start.11 = (bf16[64,1536]{1,0:T(8,128)(2,1)S(1)}, bf16[64,1536]{1,0:T(8,128)(2,1)S(1)}, u32[]{:S(2)}, u32[]{:S(2)}) collective-permute-start(bf16[64,1536]{1,0:T(8,128)(2,1)S(1)} %dynamic-slice_convert_fusion.3), channel_id=1, source_target_pairs={{0,8},{2,10},{4,12},{6,14},{8,0},{10,2},{12,4},{14,6},{16,24},{18,... | collective-permute-start | bytes 589832 | tf_op jit(solution)/shard_map/ppermute | solution.py:699
  322.3 6.9 %collective-permute-start.12 = (bf16[32,1536]{1,0:T(8,128)(2,1)S(1)}, bf16[32,1536]{1,0:T(8,128)(2,1)S(1)}, u32[]{:S(2)}, u32[]{:S(2)}) collective-permute-start(bf16[32,1536]{1,0:T(8,128)(2,1)S(1)} %dynamic-slice_convert_fusion.5), channel_id=1, source_target_pairs={{0,16},{2,18},{4,20},{6,22},{8,24},{10,26},{12,28},{14,30},{16,0},... | collective-permute-start | bytes 294920 | tf_op jit(solution)/shard_map/ppermute | solution.py:699
  324.7 6.1 %collective-permute-start.22 = (bf16[32,512]{1,0:T(8,128)(2,1)S(1)}, bf16[32,512]{1,0:T(8,128)(2,1)S(1)}, u32[]{:S(2)}, u32[]{:S(2)}) collective-permute-start(bf16[32,512]{1,0:T(8,128)(2,1)S(1)} %dynamic-slice_convert_fusion.8), channel_id=1, source_target_pairs={{0,16},{2,18},{4,20},{6,22},{8,24},{10,26},{12,28},{14,30},{16,0},... | collective-permute-start | bytes 98312 | tf_op jit(solution)/shard_map/ppermute | solution.py:699
  329.3 20.3 %collective-permute-start.13 = (bf16[16,1536]{1,0:T(8,128)(2,1)S(1)}, bf16[16,1536]{1,0:T(8,128)(2,1)S(1)}, u32[]{:S(2)}, u32[]{:S(2)}) collective-permute-start(bf16[16,1536]{1,0:T(8,128)(2,1)S(1)} %dynamic-slice_convert_fusion.7), channel_id=1, source_target_pairs={{0,1},{1,0},{2,3},{3,2},{4,5},{5,4},{6,7},{7,6},{8,9},{9,8},{10,11... | collective-permute-start | bytes 147464 | tf_op jit(solution)/shard_map/ppermute | solution.py:699
  349.6 4.2 %collective-permute-start.14 = (bf16[16,1536]{1,0:T(8,128)(2,1)S(1)}, bf16[16,1536]{1,0:T(8,128)(2,1)S(1)}, u32[]{:S(2)}, u32[]{:S(2)}) collective-permute-start(bf16[16,1536]{1,0:T(8,128)(2,1)S(1)} %add_convert_fusion), channel_id=1, source_target_pairs={{0,1},{1,0},{2,3},{3,2},{4,5},{5,4},{6,7},{7,6},{8,9},{9,8},{10,11... | collective-permute-start | bytes 147464 | tf_op jit(solution)/shard_map/ppermute | solution.py:699
  350.1 3.8 collective-permute-start.23
  353.7 2.7 collective-permute-start.4
  353.9 8.2 %collective-permute-start.15 = (bf16[32,1536]{1,0:T(8,128)(2,1)S(1)}, bf16[32,1536]{1,0:T(8,128)(2,1)S(1)}, u32[]{:S(2)}, u32[]{:S(2)}) collective-permute-start(bf16[32,1536]{1,0:T(8,128)(2,1)S(1)} %maximum_select_fusion.7), channel_id=1, source_target_pairs={{0,16},{2,18},{4,20},{6,22},{8,24},{10,26},{12,28},{14,30},{16,0},... | collective-permute-start | bytes 294920 | tf_op jit(solution)/shard_map/ppermute | solution.py:699
  356.4 7.3 %collective-permute-start.24 = (bf16[16,512]{1,0:T(8,128)(2,1)S(1)}, bf16[16,512]{1,0:T(8,128)(2,1)S(1)}, u32[]{:S(2)}, u32[]{:S(2)}) collective-permute-start(bf16[16,512]{1,0:T(8,128)(2,1)S(1)} %add_convert_fusion.1), channel_id=1, source_target_pairs={{0,1},{1,0},{2,3},{3,2},{4,5},{5,4},{6,7},{7,6},{8,9},{9,8},{10,11... | collective-permute-start | bytes 49160 | tf_op jit(solution)/shard_map/ppermute | solution.py:699
  362.0 6.9 %collective-permute-start.5 = (f32[21,512]{1,0:T(8,128)S(1)}, f32[21,512]{1,0:T(8,128)S(1)}, u32[]{:S(2)}, u32[]{:S(2)}) collective-permute-start(f32[21,512]{1,0:T(8,128)S(1)} %add.138), channel_id=1, source_target_pairs={{0,4},{2,6},{4,0},{6,2},{8,12},{10,14},{12,8},{14,10},{16,20},{18,... | collective-permute-start | bytes 129032 | tf_op jit(solution)/shard_map/ppermute | solution.py:699
  363.7 10.8 %collective-permute-start.16 = (bf16[64,1536]{1,0:T(8,128)(2,1)S(1)}, bf16[64,1536]{1,0:T(8,128)(2,1)S(1)}, u32[]{:S(2)}, u32[]{:S(2)}) collective-permute-start(bf16[64,1536]{1,0:T(8,128)(2,1)S(1)} %maximum_select_fusion.5), channel_id=1, source_target_pairs={{0,8},{2,10},{4,12},{6,14},{8,0},{10,2},{12,4},{14,6},{16,24},{18,... | collective-permute-start | bytes 589832 | tf_op jit(solution)/shard_map/ppermute | solution.py:699
  364.3 5.4 %collective-permute-start.25 = (bf16[32,512]{1,0:T(8,128)(2,1)S(1)}, bf16[32,512]{1,0:T(8,128)(2,1)S(1)}, u32[]{:S(2)}, u32[]{:S(2)}) collective-permute-start(bf16[32,512]{1,0:T(8,128)(2,1)S(1)} %maximum_select_fusion.9), channel_id=1, source_target_pairs={{0,16},{2,18},{4,20},{6,22},{8,24},{10,26},{12,28},{14,30},{16,0},... | collective-permute-start | bytes 98312 | tf_op jit(solution)/shard_map/ppermute | solution.py:699
  368.9 4.9 %collective-permute-start.6 = (f32[21,512]{1,0:T(8,128)S(1)}, f32[21,512]{1,0:T(8,128)S(1)}, u32[]{:S(2)}, u32[]{:S(2)}) collective-permute-start(f32[21,512]{1,0:T(8,128)S(1)} %add.139), channel_id=1, source_target_pairs={{0,8},{2,10},{4,12},{6,14},{8,0},{10,2},{12,4},{14,6},{16,24},{18,... | collective-permute-start | bytes 129032 | tf_op jit(solution)/shard_map/ppermute | solution.py:699
  369.7 17.9 %collective-permute-start.26 = (bf16[64,512]{1,0:T(8,128)(2,1)S(1)}, bf16[64,512]{1,0:T(8,128)(2,1)S(1)}, u32[]{:S(2)}, u32[]{:S(2)}) collective-permute-start(bf16[64,512]{1,0:T(8,128)(2,1)S(1)} %maximum_select_fusion.8), channel_id=1, source_target_pairs={{0,8},{2,10},{4,12},{6,14},{8,0},{10,2},{12,4},{14,6},{16,24},{18,... | collective-permute-start | bytes 196616 | tf_op jit(solution)/shard_map/ppermute | solution.py:699
  373.8 11.7 %collective-permute-start.7 = (f32[21,512]{1,0:T(8,128)S(1)}, f32[21,512]{1,0:T(8,128)S(1)}, u32[]{:S(2)}, u32[]{:S(2)}) collective-permute-start(f32[21,512]{1,0:T(8,128)S(1)} %add.140), channel_id=1, source_target_pairs={{0,16},{2,18},{4,20},{6,22},{8,24},{10,26},{12,28},{14,30},{16,0},... | collective-permute-start | bytes 129032 | tf_op jit(solution)/shard_map/ppermute | solution.py:699
  374.6 24.9 %collective-permute-start.17 = (bf16[128,1536]{1,0:T(8,128)(2,1)S(1)}, bf16[128,1536]{1,0:T(8,128)(2,1)S(1)}, u32[]{:S(2)}, u32[]{:S(2)}) collective-permute-start(bf16[128,1536]{1,0:T(8,128)(2,1)S(1)} %maximum_select_fusion.3), channel_id=1, source_target_pairs={{0,4},{2,6},{4,0},{6,2},{8,12},{10,14},{12,8},{14,10},{16,20},{18,... | collective-permute-start | bytes 1179656 | tf_op jit(solution)/shard_map/ppermute | solution.py:699
  385.5 18.0 %collective-permute-start.3 = (bf16[2,256,512]{2,1,0:T(8,128)(2,1)S(1)}, bf16[2,256,512]{2,1,0:T(8,128)(2,1)S(1)}, u32[]{:S(2)}, u32[]{:S(2)}) collective-permute-start(bf16[2,256,512]{2,1,0:T(8,128)(2,1)S(1)} %copy-done.23), channel_id=1, source_target_pairs={{0,1},{1,0},{2,3},{3,2},{4,5},{5,4},{6,7},{7,6},{8,9},{9,8},{10,11... | collective-permute-start | bytes 1572872 | tf_op jit(solution)/shard_map/ppermute | solution.py:699
  385.5 18.0 %copy-start.3 = (f32[1024,512]{1,0:T(8,128)S(1)}, f32[1024,512]{1,0:T(8,128)}, u32[]{:S(2)}) copy-start(f32[1024,512]{1,0:T(8,128)} %get-tuple-element.48.resid_ref) | copy-start | bytes 6291460
  385.6 18.0 %copy-start.9 = (bf16[2,256,512]{2,1,0:T(8,128)(2,1)S(1)}, bf16[2,256,512]{2,1,0:T(8,128)(2,1)}, u32[]{:S(2)}) copy-start(bf16[2,256,512]{2,1,0:T(8,128)(2,1)} %copy-done.8) | copy-start | bytes 1572868
  385.6 13.3 %collective-permute-start.8 = (f32[21,512]{1,0:T(8,128)S(1)}, f32[21,512]{1,0:T(8,128)S(1)}, u32[]{:S(2)}, u32[]{:S(2)}) collective-permute-start(f32[21,512]{1,0:T(8,128)S(1)} %add.141), channel_id=1, source_target_pairs={{0,1},{1,0},{2,3},{3,2},{4,5},{5,4},{6,7},{7,6},{8,9},{9,8},{10,11... | collective-permute-start | bytes 129032 | tf_op jit(solution)/shard_map/ppermute | solution.py:699
  387.7 12.2 %collective-permute-start.27 = (bf16[128,512]{1,0:T(8,128)(2,1)S(1)}, bf16[128,512]{1,0:T(8,128)(2,1)S(1)}, u32[]{:S(2)}, u32[]{:S(2)}) collective-permute-start(bf16[128,512]{1,0:T(8,128)(2,1)S(1)} %maximum_select_fusion.6), channel_id=1, source_target_pairs={{0,4},{2,6},{4,0},{6,2},{8,12},{10,14},{12,8},{14,10},{16,20},{18,... | collective-permute-start | bytes 393224 | tf_op jit(solution)/shard_map/ppermute | solution.py:699
  399.6 5.9 %collective-permute-start.18 = (bf16[256,1536]{1,0:T(8,128)(2,1)S(1)}, bf16[256,1536]{1,0:T(8,128)(2,1)S(1)}, u32[]{:S(2)}, u32[]{:S(2)}) collective-permute-start(bf16[256,1536]{1,0:T(8,128)(2,1)S(1)} %maximum_select_fusion.1), channel_id=1, source_target_pairs={{0,2},{2,0},{4,6},{6,4},{8,10},{10,8},{12,14},{14,12},{16,18},{18,... | collective-permute-start | bytes 2359304 | tf_op jit(solution)/shard_map/ppermute | solution.py:699
  399.9 2.5 collective-permute-start.28
  (31 other events, 84.1 us)

commit v2 on v1

--- a/solution.py
+++ b/solution.py
@@ -16,6 +16,7 @@
 BF16 = jnp.bfloat16
 F32 = jnp.float32
 MIB = 1 << 20
+SMALL = 128
 
 
 def normalize(values):
@@ -148,6 +149,11 @@
     )(flag, inputs, far, gain, w_qkv_t)
 
 
+def small_columns(small, gain):
+    rest = jnp.zeros((SMALL - small.shape[0] - 1, small.shape[1]), F32)
+    return jnp.concatenate([small, gain, rest], 0).T
+
+
 def attend_back_kernel(
     flag_ref,
     own_ref,
@@ -158,15 +164,17 @@
     total_ref,
     d_own_ref,
     d_far_ref,
+    attn_ref,
+    small_ref,
     own_out,
     far_out,
-    weight_out,
-    gain_out,
+    keep_out,
+    send_out,
     d_proj,
     d_mixed,
     weight_sum,
+    gain_out,
 ):
-    del flag_ref
     image, last = pl.program_id(0), pl.num_programs(0) - 1
     rows, width = own_ref.shape[1], own_ref.shape[2]
     head_dim = width // HEADS
@@ -212,10 +220,17 @@
 
     @pl.when(image == last)
     def finish():
-        weight_out[...] = weight_sum[...].T
-
-
-def attend_back(flag, inputs, far, gain, w_qkv_t, proj, total, d_heads, d_far):
+        half = width // 2
+        parts = ((weight_sum[...].T, 0), (attn_ref[...], 3 * width))
+        parts += ((small_columns(small_ref[...], gain_out[...]), 4 * width),)
+        upper = flag_ref[1] == 1
+        for value, at in parts:
+            at = slice(at, at + value.shape[1])
+            keep_out[:, at] = jnp.where(upper, value[half:], value[:half])
+            send_out[:, at] = jnp.where(upper, value[:half], value[half:]).astype(BF16)
+
+
+def attend_back(flag, inputs, far, gain, w_qkv_t, proj, total, d_heads, d_far, attn_term, small):
     part, rows, width = far.shape
     seq_len = 2 * rows
     block = lambda *shape: pl.BlockSpec((1,) + shape, lambda i, flag_ref: (i,) + (0,) * len(shape))
@@ -233,29 +248,32 @@
                 block(HEADS, seq_len),
                 block(rows, width),
                 block(rows, width),
+                whole(attn_term.shape),
+                whole(small.shape),
             ],
             out_specs=[
                 block(rows, width),
                 block(rows, width),
-                whole((width, 3 * width)),
-                whole((1, width)),
+                whole((width // 2, 4 * width + SMALL)),
+                whole((width // 2, 4 * width + SMALL)),
             ],
             scratch_shapes=[
                 pltpu.VMEM((3 * width, seq_len), BF16),
                 pltpu.VMEM((width, seq_len), BF16),
                 pltpu.VMEM((3 * width, width), F32),
+                pltpu.VMEM((1, width), F32),
             ],
         ),
         out_shape=[
             jax.ShapeDtypeStruct((part, rows, width), BF16),
             jax.ShapeDtypeStruct((part, rows, width), BF16),
-            jax.ShapeDtypeStruct((width, 3 * width), F32),
-            jax.ShapeDtypeStruct((1, width), F32),
+            jax.ShapeDtypeStruct((width // 2, 4 * width + SMALL), F32),
+            jax.ShapeDtypeStruct((width // 2, 4 * width + SMALL), BF16),
         ],
-        compiler_params=params(48),
+        compiler_params=params(60),
         cost_estimate=cost(part * 16e9, 12 * MIB, part * HEADS * seq_len**2),
         name="attend_back",
-    )(flag, inputs, far, gain, w_qkv_t, proj, total, d_heads, d_far)
+    )(flag, inputs, far, gain, w_qkv_t, proj, total, d_heads, d_far, attn_term, small)
 
 
 def residual_kernel(
@@ -465,7 +483,7 @@
         out_specs=pl.BlockSpec((width, block), lambda i: (0, i)),
         out_shape=jax.ShapeDtypeStruct((width, hidden_width), BF16),
         scratch_shapes=[pltpu.VMEM((width, total), BF16)],
-        compiler_params=params(40),
+        compiler_params=params(60),
         cost_estimate=cost(2 * total * width * hidden_width, 14 * MIB),
         name="weight_grad",
     )(left, right)
@@ -685,42 +703,131 @@
     )(flag, d_resid, own, far)
 
 
+AXES = ("wide", "narrow")
+
+
+def device_bits():
+    n_narrow = lax.axis_size("narrow")
+    masks = [1 << b for b in range((n_narrow * lax.axis_size("wide")).bit_length() - 1)]
+    masks.remove(n_narrow)
+    return [n_narrow] + masks
+
+
 def sum_steps():
-    steps = []
-    for axis in ("wide", "narrow"):
-        bit = 1
-        while bit < lax.axis_size(axis):
-            steps.append((axis, bit))
-            bit *= 2
-    return steps
-
-
-def swap(value, axis, bit):
-    return lax.ppermute(value, axis, [(i, i ^ bit) for i in range(lax.axis_size(axis))])
-
-
-def sum_all(value):
-    steps = sum_steps()
-    for axis, bit in steps:
-        half = value.shape[0] // 2
-        side = (lax.axis_index(axis) // bit) % 2
-        keep = lax.dynamic_slice_in_dim(value, side * half, half, 0)
-        send = lax.dynamic_slice_in_dim(value, (1 - side) * half, half, 0).astype(BF16)
-        value = keep + swap(send, axis, bit).astype(F32)
-    value = value.astype(BF16)
-    for axis, bit in reversed(steps):
-        side = (lax.axis_index(axis) // bit) % 2
-        far = swap(value, axis, bit)
-        value = jnp.where(
-            side == 0, jnp.concatenate([value, far], 0), jnp.concatenate([far, value], 0)
-        )
-    return value.astype(F32)
-
-
-def sum_small(value):
-    for axis, bit in sum_steps():
-        value = value + swap(value, axis, bit)
-    return value
+    first, *rest = device_bits()
+    return [(first,)] + [tuple(rest[i : i + 2]) for i in range(0, len(rest), 2)]
+
+
+def swap(value, mask, axes=AXES):
+    size = math.prod(lax.axis_size(axis) for axis in axes)
+    return lax.ppermute(value, axes, [(i, i ^ mask) for i in range(size)])
+
+
+def partners(bits):
+    me = lax.axis_index(AXES)
+    place = sum(((me // bit) % 2) << b for b, bit in enumerate(bits))
+    masks = [
+        sum(bit for b, bit in enumerate(bits) if (j >> b) & 1) for j in range(1 << len(bits))
+    ]
+    return masks, place
+
+
+def fold_kernel(given, members, place_ref, keep_ref, *refs):
+    del place_ref
+    step = pl.program_id(0)
+    total = keep_ref[...]
+    for far_ref in refs[:given]:
+        total += far_ref[...].astype(F32)
+    own_out, *send_outs = refs[given:]
+
+    @pl.when(step == 0)
+    def keep():
+        own_out[...] = total
+
+    for j, send_out in enumerate(send_outs):
+
+        @pl.when(step == j + 1)
+        def send():
+            send_out[...] = total.astype(BF16)
+
+
+def fold(keep, far, bits):
+    masks, place = partners(bits)
+    members = len(masks)
+    rows, size = keep.shape
+    part = rows // members
+    pick = pl.BlockSpec((part, size), lambda j, place_ref: (place_ref[0] ^ j, 0))
+    own, *send = pl.pallas_call(
+        functools.partial(fold_kernel, len(far), members),
+        grid_spec=pltpu.PrefetchScalarGridSpec(
+            num_scalar_prefetch=1,
+            grid=(members,),
+            in_specs=[pick] * (1 + len(far)),
+            out_specs=[whole((part, size))] * members,
+        ),
+        out_shape=[jax.ShapeDtypeStruct((part, size), F32)]
+        + [jax.ShapeDtypeStruct((part, size), BF16)] * (members - 1),
+        compiler_params=params(32),
+        cost_estimate=cost(0, 8 * rows * size),
+        name="fold",
+    )(place.reshape(1).astype(jnp.int32), keep, *far)
+    return own, [swap(value, mask) for value, mask in zip(send, masks[1:])]
+
+
+def sum_parts(value, bits):
+    masks, place = partners(bits)
+    part = value.shape[0] // len(masks)
+    pick = lambda j: lax.dynamic_slice_in_dim(value, (place ^ j) * part, part, 0)
+    far = [swap(pick(j).astype(BF16), masks[j]) for j in range(1, len(masks))]
+    total = pick(0)
+    for term in far:
+        total = total + term.astype(F32)
+    return total
+
+
+def spread_parts(value, bits):
+    masks, place = partners(bits)
+    parts = [value] + [swap(value, mask) for mask in masks[1:]]
+    for b in range(len(bits)):
+        side = (place >> b) % 2 == 0
+        parts = [
+            jnp.where(
+                side,
+                jnp.concatenate([parts[i], parts[i + 1]], 0),
+                jnp.concatenate([parts[i + 1], parts[i]], 0),
+            )
+            for i in range(0, len(parts), 2)
+        ]
+    return parts[0]
+
+
+def sums_kernel(flag_ref, own_ref, far_ref, qkv_out, attn_out, small_out):
+    half, width = own_ref.shape[0], attn_out.shape[1]
+    upper = flag_ref[1] == 1
+    own, far = own_ref[...].astype(F32), far_ref[...].astype(F32)
+    for rows, value in ((0, jnp.where(upper, far, own)), (half, jnp.where(upper, own, far))):
+        rows = slice(rows, rows + half)
+        qkv_out[rows, :] = value[:, : 3 * width]
+        attn_out[rows, :] = value[:, 3 * width : 4 * width]
+        small_out[rows, :] = value[:, 4 * width :]
+
+
+def sums_apart(flag, own, far):
+    width = 2 * own.shape[0]
+    shapes = [(width, 3 * width), (width, width), (width, SMALL)]
+    return pl.pallas_call(
+        sums_kernel,
+        grid_spec=pltpu.PrefetchScalarGridSpec(
+            num_scalar_prefetch=1,
+            grid=(1,),
+            in_specs=[whole(own.shape), whole(far.shape)],
+            out_specs=[whole(shape) for shape in shapes],
+        ),
+        out_shape=[jax.ShapeDtypeStruct(shape, F32) for shape in shapes],
+        compiler_params=params(32),
+        cost_estimate=cost(0, 8 * MIB),
+        name="sums_apart",
+    )(flag, own, far)
 
 
 def gathered_attention(inputs, gain_one, w_qkv):
@@ -824,12 +931,7 @@
     paired = n_narrow == 2 and images % 2 == 0
     part = images // 2
     place = lax.axis_index("narrow") if paired else jnp.int32(0)
-    flag = place.reshape(1)
-
-    if paired:
-        far_inputs = swap(
-            lax.dynamic_slice_in_dim(inputs, (1 - place) * part, part, 0), "narrow", 1
-        )
+    flag = jnp.stack([place, lax.axis_index("wide") % 2])
 
     slot_columns = jnp.where(
         route_dropped == 0, route_ids * slots + route_slots, -1
@@ -842,14 +944,20 @@
             rows.reshape(experts, slots, width), "wide", split_axis=0, concat_axis=0, tiled=True
         ).reshape(total, width)
 
-    up_here = exchange(dispatch_rows(slot_rows, up, total))
-
     if paired:
+        sent = lax.dynamic_slice_in_dim(inputs, (1 - place) * part, part, 0)
+        far_inputs = swap(sent, 1)
         w_qkv_t = w_qkv.T
+    up_rows = dispatch_rows(slot_rows, up, total)
+    if paired:
+        far_inputs, up_rows, w_qkv_t = lax.optimization_barrier((far_inputs, up_rows, w_qkv_t))
+    up_here = exchange(up_rows)
+
+    if paired:
         heads_own, heads_far, proj, log_total = attend(
             flag, inputs, far_inputs, gain_one, w_qkv_t
         )
-        heads_far = swap(heads_far, "narrow", 1)
+        heads_far = swap(heads_far, 1)
     else:
         heads_own, attention_back = gathered_attention(inputs, gain_one, w_qkv)
         heads_own, heads_far = heads_own[:part], heads_own[part:]
@@ -873,19 +981,11 @@
         slots,
     )
     back = exchange(back)
-    y = exchange(y)
     grad_out_t = weight_grad(d_y, act)
     grad_in = weight_grad(rows_here, d_hidden)
-    biases = jnp.concatenate([b_in_sum, b_out_sum], 1)
+    back, *unused = lax.optimization_barrier((back, grad_out_t, grad_in))
     if n_narrow == 2:
-        grad_expert_out = turned_sum(grad_out_t, swap(grad_out_t, "narrow", 1))
-        grad_expert_in = grad_in.astype(F32) + swap(grad_in, "narrow", 1).astype(F32)
-        biases = biases + swap(biases, "narrow", 1)
-    else:
-        grad_out_t, grad_in = lax.psum((grad_out_t, grad_in), "narrow")
-        grad_expert_out = grad_out_t.astype(F32).T
-        grad_expert_in = grad_in.astype(F32)
-        biases = lax.psum(biases, "narrow")
+        far_out_t = swap(grad_out_t, 1)
 
     d_resid, d_heads, attn_term, router_term, gain_two_term = token_back(
         flag,
@@ -905,30 +1005,84 @@
         part,
     )
     d_heads = d_heads.reshape(images, rows_dev, width)
+    sent, y, grad_in = lax.optimization_barrier((d_heads[part:], y, grad_in))
+    biases = jnp.concatenate([b_in_sum, b_out_sum], 1)
+    small = jnp.concatenate([router_term, gain_two_term, moments], 0)
+    steps = sum_steps()
     if paired:
-        d_far = swap(d_heads[part:], "narrow", 1)
-        d_own, d_far, qkv_term, gain_one_term = attend_back(
-            flag, inputs, far_inputs, gain_one, w_qkv_t, proj, log_total, d_heads, d_far
+        d_far = swap(sent, 1)
+        far_in = swap(grad_in, 1)
+        far_biases = swap(biases, 1)
+        y = exchange(y)
+        d_far, far_out_t = lax.optimization_barrier((d_far, far_out_t))
+        d_own, d_far, keep, send = attend_back(
+            flag,
+            inputs,
+            far_inputs,
+            gain_one,
+            w_qkv_t,
+            proj,
+            log_total,
+            d_heads,
+            d_far,
+            attn_term,
+            small,
         )
-        input_grad = grad_sum(flag, d_resid, d_own, swap(d_far, "narrow", 1))
+        keep, send, d_far, far_out_t = lax.optimization_barrier((keep, send, d_far, far_out_t))
+        grad_expert_out = turned_sum(grad_out_t, far_out_t)
+        keep, send, d_far, far_in, grad_expert_out = lax.optimization_barrier(
+            (keep, send, d_far, far_in, grad_expert_out)
+        )
+        sums, far = fold(keep, [swap(send, steps[0][0])], steps[1])
+        grad_expert_in = grad_in.astype(F32) + far_in.astype(F32)
+        sums, far, y, d_far, grad_expert_in, far_biases = lax.optimization_barrier(
+            (sums, far, y, d_far, grad_expert_in, far_biases)
+        )
+        d_far = swap(d_far, 1)
+        biases = biases + far_biases
+        for bits in steps[2:]:
+            sums, far = fold(sums, far, bits)
+        for term in far:
+            sums = sums + term.astype(F32)
     else:
+        y = exchange(y)
+        grad_out_t, grad_in = lax.psum((grad_out_t, grad_in), "narrow")
+        grad_expert_out = grad_out_t.astype(F32).T
+        grad_expert_in = grad_in.astype(F32)
+        biases = lax.psum(biases, "narrow")
         input_grad, qkv_term, gain_one_term = attention_back(d_heads, d_resid)
-
+        small = small_columns(small, gain_one_term)
+        sums = jnp.concatenate([qkv_term, attn_term, small], 1)
+        for bits in steps:
+            sums = sum_parts(sums, bits)
     block_out, moe_moment = combine_rows(slot_columns, y, resid, rows_dev)
-    small = jnp.concatenate([router_term, gain_one_term, gain_two_term, moments, moe_moment], 0)
-    small = sum_small(small)
-    grad_attn_out = sum_all(attn_term)
-    grad_qkv = sum_all(qkv_term)
+    moe_moment = jnp.sum(moe_moment)
+    high = moe_moment.astype(BF16).astype(F32)
+    row = lax.broadcasted_iota(jnp.int32, sums.shape, 0)
+    lane = lax.broadcasted_iota(jnp.int32, sums.shape, 1) - 4 * width - (experts + 4)
+    extra = jnp.where(lane == 0, high, jnp.where(lane == 1, moe_moment - high, 0.0))
+    sums = jnp.where((row == 0) & (lane >= 0), extra, sums).astype(BF16)
+    for bits in reversed(steps[2:]):
+        sums = spread_parts(sums, bits)
+    if paired:
+        sums, d_far, block_out = lax.optimization_barrier((sums, d_far, block_out))
+        input_grad = grad_sum(flag, d_resid, d_own, d_far)
+    sums = spread_parts(sums, steps[1])
+    if paired:
+        sums, input_grad = lax.optimization_barrier((sums, input_grad))
+    grad_qkv, grad_attn_out, small = sums_apart(flag, sums, swap(sums, steps[0][0]))
     moment_count = tokens * width * n_wide * n_narrow
-    stats = jnp.sqrt(jnp.sum(small[experts + 2 : experts + 5], 1) / moment_count + EPS)
+    moments = jnp.sum(small[:, experts + 1 : experts + 6], 0)
+    moments = jnp.stack([moments[0], moments[1], moments[3] + moments[4]])
+    stats = jnp.sqrt(moments / moment_count + EPS)
     return (
         block_out.reshape(images, rows_dev, width),
         input_grad.reshape(images, rows_dev, width),
-        small[experts],
+        small[:, experts + 3],
         grad_qkv,
         grad_attn_out,
-        small[experts + 1],
-        small[:experts].T,
+        small[:, experts],
+        small[:, :experts],
         grad_expert_in[None],
         biases[:, : w_in.shape[1]],
         grad_expert_out[None],

time: 409 us -> 373 us (0.912)
  waiting for transfers between devices: 156 us -> 116 us
  Pallas kernels: 122 us -> 140 us
  local copies, waits for them, and re-layouts: 39.6 us -> 29.2 us
    all_to_all x4, waiting for transfers between devices: 86.2 us -> 66.1 us  [exchange(): lax.all_to_all(rows.reshape(experts, slots, width), 'wide', split_axis=0,...]
    ppermute x32 -> x21, waiting for transfers between devices: 69.4 us -> 50 us  [swap(): return lax.ppermute(value, axes, [(i, i ^ mask) for i in range(size)])]
    unnamed x89 -> x74, local copies, waits for them, and re-layouts: 32 us -> 23.4 us
    ppermute x32 -> x21, starting transfers between devices: 39.3 us -> 31.8 us  [swap(): return lax.ppermute(value, axes, [(i, i ^ mask) for i in range(size)])]
    pallas_call x0 -> x3, Pallas kernels: none -> 6.16 us  [the longest x2 3.14 us: fold(): pl.pallas_call(functools.partial(fold_kernel, len(far), members), grid_sp...]
    broadcast_in_dim x1 -> x0, other arithmetic: 5.05 us -> none  [shards(): grad_expert_in[None]]
    all_to_all x4, starting transfers between devices: 36.8 us -> 41.8 us  [exchange(): lax.all_to_all(rows.reshape(experts, slots, width), 'wide', split_axis=0,...]
    pallas_call x2, Pallas kernels: 15.5 us -> 19.9 us  [weight_grad(): pl.pallas_call(weight_kernel, grid=(hidden_width // block,), in_specs=[wh...]
  transfers between devices with their start and end apart: 36 -> 25, of which waited for: 14 -> 16; matrix products, arithmetic and copies ran while one was open for 4% -> 3% of each run, Pallas kernels for 18% -> 28%
where the time goes in v2:
time: 373 us; the launch traced here: 372 us
  Pallas kernels  140 us (38%)
  waiting for transfers between devices  116 us (31%)
  starting transfers between devices  73.5 us (20%)
  local copies, waits for them, and re-layouts  29.2 us (8%)
  other arithmetic  9.45 us (3%)
    all_to_all x4, waiting for transfers between devices, exchange(): lax.all_to_all(rows.reshape(experts, slots, width), 'wide', split_axis=0,...  66.1 us
    ppermute x21, waiting for transfers between devices, swap(): return lax.ppermute(value, axes, [(i, i ^ mask) for i in range(size)])  50 us
    all_to_all x4, starting transfers between devices, exchange(): lax.all_to_all(rows.reshape(experts, slots, width), 'wide', split_axis=0,...  41.8 us
    ppermute x21, starting transfers between devices, swap(): return lax.ppermute(value, axes, [(i, i ^ mask) for i in range(size)])  31.8 us
    pallas_call x1, Pallas kernels, expert_rows(): pl.pallas_call(functools.partial(expert_kernel, capacity, slots), grid=(s...  31.2 us
    pallas_call x1, Pallas kernels, attend_back(): pl.pallas_call(attend_back_kernel, grid_spec=pltpu.PrefetchScalarGridSpec...  28.9 us
    unnamed x74, local copies, waits for them, and re-layouts  23.4 us
    pallas_call x2, Pallas kernels, weight_grad(): pl.pallas_call(weight_kernel, grid=(hidden_width // block,), in_specs=[wh...  19.9 us
  transfers between devices with their start and end apart: 25, of which 16 were waited for; matrix products, arithmetic and copies ran while one was open for 3% of the time, Pallas kernels for 28%

profile of v2, /device:TPU:0, one launch (start us, length us, event | category | flops | bytes accessed | tf_op | source)
XLA Modules:
  0.0 371.8 jit_solution(5599889976729065206)
XLA Ops:
  0.6 1.9 constant_dynamic-slice_fusion
  2.5 3.0 collective-permute-start
  6.7 1.7 copy.35
  8.4 5.2 %dispatch_rows.1 = bf16[2176,512]{1,0:T(8,128)(2,1)} custom-call(s32[2,1024]{1,0:T(2,128)S(1)} %copy.34.slots_ref.lines_ref, bf16[1024,512]{1,0:T(8,128)(2,1)S(1)} %bitcast.46), custom_call_target="tpu_custom_call" | custom-call | flops 2281701376 | bytes 4456448 | tf_op jit(solution)/shard_map/dispatch_rows/pallas_call | solution.py:73
  13.6 4.1 %collective-permute-done.far_ref = bf16[2,256,512]{2,1,0:T(8,128)(2,1)} collective-permute-done((bf16[2,256,512]{2,1,0:T(8,128)(2,1)}, bf16[2,256,512]{2,1,0:T(8,128)(2,1)}, u32[]{:S(2)}, u32[]{:S(2)}) %collective-permute-start) | collective-permute-done | bytes 524320 | tf_op jit(solution)/shard_map/ppermute | solution.py:723
  17.7 6.3 %all-to-all-start.1 = ((bf16[16,136,512]{2,1,0:T(8,128)(2,1)}), bf16[16,136,512]{2,1,0:T(8,128)(2,1)}, u32[]{:S(2)}, u32[]{:S(2)}) async-start(bf16[16,136,512]{2,1,0:T(8,128)(2,1)} %bitcast.11), calls=%async_computation.1 | async-start | bytes 4456448 | tf_op jit(solution)/shard_map/all_to_all | solution.py:943
  24.2 15.7 %attend.1 = (bf16[2,256,512]{2,1,0:T(8,128)(2,1)S(1)}, bf16[2,256,512]{2,1,0:T(8,128)(2,1)S(1)}, bf16[2,1536,512]{2,1,0:T(8,128)(2,1)S(1)}, f32[2,8,512]{2,1,0:T(8,128)S(1)}) custom-call(s32[2]{0:T(128)S(1)} %pad_add_fusion.flag_ref, bf16[4,256,512]{2,1,0:T(8,128)(2,1)S(1)} %copy-done.12, bf16[2,256,512]{2,1,0:T(8,128)(2,1)} %collective-permute-done.far_ref, ...), custom_call_target="tpu_custom_call" | custom-call | flops 16000000000 | bytes 8388608 | tf_op jit(solution)/shard_map/attend/pallas_call | solution.py:121
  40.0 1.7 copy-done.29
  42.2 1.5 collective-permute-start.1
  43.8 12.6 %collective-permute-done.1.far_ref = bf16[2,256,512]{2,1,0:T(8,128)(2,1)S(1)} collective-permute-done((bf16[2,256,512]{2,1,0:T(8,128)(2,1)S(1)}, bf16[2,256,512]{2,1,0:T(8,128)(2,1)S(1)}, u32[]{:S(2)}, u32[]{:S(2)}) %collective-permute-start.1) | collective-permute-done | bytes 524320 | tf_op jit(solution)/shard_map/ppermute | solution.py:723
  56.4 7.1 %residual_rows.1 = (bf16[1024,512]{1,0:T(8,128)(2,1)S(1)}, f32[1024,512]{1,0:T(8,128)S(1)}, bf16[1024,512]{1,0:T(8,128)(2,1)S(1)}, bf16[2176,512]{1,0:T(8,128)(2,1)}, f32[2,512]{1,0:T(2,128)S(1)}) custom-call(s32[2]{0:T(128)S(1)} %pad_add_fusion.flag_ref, bf16[2,256,512]{2,1,0:T(8,128)(2,1)S(1)} %get-tuple-element.85.own_ref, ...), custom_call_target="tpu_custom_call" | custom-call | flops 2818572288 | bytes 10485760 | tf_op jit(solution)/shard_map/residual_rows/pallas_call | solution.py:320
  67.5 11.9 %all-to-all-start = ((bf16[16,136,512]{2,1,0:T(8,128)(2,1)}), bf16[16,136,512]{2,1,0:T(8,128)(2,1)}, u32[]{:S(2)}, u32[]{:S(2)}) async-start(bf16[16,136,512]{2,1,0:T(8,128)(2,1)} %bitcast.9), calls=%async_computation | async-start | bytes 4456448 | tf_op jit(solution)/shard_map/all_to_all | solution.py:943
  79.6 43.3 %all-to-all-done = bf16[16,136,512]{2,1,0:T(8,128)(2,1)} async-done(((bf16[16,136,512]{2,1,0:T(8,128)(2,1)}), bf16[16,136,512]{2,1,0:T(8,128)(2,1)}, u32[]{:S(2)}, u32[]{:S(2)}) %all-to-all-start) | async-done | bytes 2228256 | tf_op jit(solution)/shard_map/all_to_all | solution.py:943
  122.9 1.6 copy-done.18
  124.5 31.2 %expert_rows.1 = (bf16[2176,512]{1,0:T(8,128)(2,1)}, bf16[2176,512]{1,0:T(8,128)(2,1)}, bf16[2176,2048]{1,0:T(8,128)(2,1)}, bf16[2176,2048]{1,0:T(8,128)(2,1)}, ...) custom-call(bf16[2176,512]{1,0:T(8,128)(2,1)} %bitcast.10.rows_ref.left_ref, ...), custom_call_target="tpu_custom_call" | custom-call | flops 18253611008 | bytes 33554432 | tf_op jit(solution)/shard_map/expert_rows/pallas_call | solution.py:431
  155.7 11.8 %all-to-all-start.2 = ((bf16[16,136,512]{2,1,0:T(8,128)(2,1)}), bf16[16,136,512]{2,1,0:T(8,128)(2,1)}, u32[]{:S(2)}, u32[]{:S(2)}) async-start(bf16[16,136,512]{2,1,0:T(8,128)(2,1)} %bitcast.50), calls=%async_computation.2 | async-start | bytes 4456448 | tf_op jit(solution)/shard_map/all_to_all | solution.py:943
  167.5 9.9 %weight_grad.2.own_ref = bf16[512,2048]{1,0:T(8,128)(2,1)} custom-call(bf16[2176,512]{1,0:T(8,128)(2,1)} %get-tuple-element.90.left_ref, bf16[2176,2048]{1,0:T(8,128)(2,1)} %get-tuple-element.91.right_ref), custom_call_target="tpu_custom_call" | custom-call | flops 4563402752 | bytes 14680064 | tf_op jit(solution)/shard_map/weight_grad/pallas_call | solution.py:479
  177.3 1.5 collective-permute-start.3
  178.9 10.0 %weight_grad.3 = bf16[512,2048]{1,0:T(8,128)(2,1)} custom-call(bf16[2176,512]{1,0:T(8,128)(2,1)} %bitcast.10.rows_ref.left_ref, bf16[2176,2048]{1,0:T(8,128)(2,1)} %get-tuple-element.92.right_ref), custom_call_target="tpu_custom_call" | custom-call | flops 4563402752 | bytes 14680064 | tf_op jit(solution)/shard_map/weight_grad/pallas_call | solution.py:479
  188.9 22.0 %all-to-all-done.2 = bf16[16,136,512]{2,1,0:T(8,128)(2,1)} async-done(((bf16[16,136,512]{2,1,0:T(8,128)(2,1)}), bf16[16,136,512]{2,1,0:T(8,128)(2,1)}, u32[]{:S(2)}, u32[]{:S(2)}) %all-to-all-start.2) | async-done | bytes 2228256 | tf_op jit(solution)/shard_map/all_to_all | solution.py:943
  212.1 14.5 %token_back.1 = (f32[1024,512]{1,0:T(8,128)}, bf16[1024,512]{1,0:T(8,128)(2,1)S(1)}, f32[512,512]{1,0:T(8,128)S(1)}, f32[16,512]{1,0:T(8,128)S(1)}, f32[1,512]{1,0:T(1,128)S(1)}) custom-call(s32[2]{0:T(128)S(1)} %pad_add_fusion.flag_ref, s32[1024,2]{1,0:T(8,128)S(1)} %bitcast.33, s32[2,1024]{1,0:T(2,128)S(1)} %copy.34.slots_ref.lines_ref, ...), custom_call_target="tpu_custom_call" | custom-call | flops 3355443200 | bytes 14680064 | tf_op jit(solution)/shard_map/token_back/pallas_call | solution.py:628
  230.4 11.7 %all-to-all-start.3 = ((bf16[16,136,512]{2,1,0:T(8,128)(2,1)}), bf16[16,136,512]{2,1,0:T(8,128)(2,1)S(1)}, u32[]{:S(2)}, u32[]{:S(2)}) async-start(bf16[16,136,512]{2,1,0:T(8,128)(2,1)} %bitcast.49), calls=%async_computation.3 | async-start | bytes 4456448 | tf_op jit(solution)/shard_map/all_to_all | solution.py:943
  243.5 28.9 %attend_back.1 = (bf16[2,256,512]{2,1,0:T(8,128)(2,1)}, bf16[2,256,512]{2,1,0:T(8,128)(2,1)}, f32[256,2176]{1,0:T(8,128)}, bf16[256,2176]{1,0:T(8,128)(2,1)}) custom-call(s32[2]{0:T(128)} %copy-done.15, bf16[4,256,512]{2,1,0:T(8,128)(2,1)} %own_ref.3, bf16[2,256,512]{2,1,0:T(8,128)(2,1)} %collective-permute-done.far_ref, f32[1,512]{1,0:T(1,128)} %bitcast.40, ...), custom_call_target="tpu_custom_call" | custom-call | flops 32000000000 | bytes 12582912 | tf_op jit(solution)/shard_map/attend_back/pallas_call | solution.py:237
  272.5 1.6 copy-done.2
  274.0 4.8 %turned_sum.1 = f32[2048,512]{1,0:T(8,128)} custom-call(bf16[512,2048]{1,0:T(8,128)(2,1)S(1)} %copy-done.2, bf16[512,2048]{1,0:T(8,128)(2,1)} %collective-permute-done.3.far_ref), custom_call_target="tpu_custom_call" | custom-call | flops 1048576 | bytes 8388608 | tf_op jit(solution)/shard_map/turned_sum/pallas_call | solution.py:498
  278.9 9.4 %collective-permute-done.4 = bf16[512,2048]{1,0:T(8,128)(2,1)} collective-permute-done((bf16[512,2048]{1,0:T(8,128)(2,1)}, bf16[512,2048]{1,0:T(8,128)(2,1)}, u32[]{:S(2)}, u32[]{:S(2)}) %collective-permute-start.4) | collective-permute-done | bytes 2097184 | tf_op jit(solution)/shard_map/ppermute | solution.py:723
  288.3 1.6 collective-permute-start.9
  291.4 1.6 copy-done
  293.0 2.2 fold.2
  295.2 1.6 collective-permute-start.6
  296.8 3.6 collective-permute-start.7
  300.4 5.1 %convert_add_fusion = f32[512,2048]{1,0:T(8,128)} fusion(bf16[512,2048]{1,0:T(8,128)(2,1)} %collective-permute-done.4, bf16[512,2048]{1,0:T(8,128)(2,1)} %weight_grad.3), kind=kLoop, calls=%fused_computation | loop fusion | flops 3145728 | bytes 8388608 | tf_op jit(solution)/shard_map/add | solution.py:1037
  306.2 1.7 collective-permute-done.7.refs_1_
  308.6 4.4 %collective-permute-done.8.refs_2_ = bf16[64,2176]{1,0:T(8,128)(2,1)S(1)} collective-permute-done((bf16[64,2176]{1,0:T(8,128)(2,1)S(1)}, bf16[64,2176]{1,0:T(8,128)(2,1)S(1)}, u32[]{:S(2)}, u32[]{:S(2)}) %collective-permute-start.8) | collective-permute-done | bytes 278560 | tf_op jit(solution)/shard_map/ppermute | solution.py:723
  317.4 6.9 %collective-permute-start.12 = (bf16[16,2176]{1,0:T(8,128)(2,1)}, bf16[16,2176]{1,0:T(8,128)(2,1)}, u32[]{:S(2)}, u32[]{:S(2)}) collective-permute-start(bf16[16,2176]{1,0:T(8,128)(2,1)} %get-tuple-element.134), channel_id=1, source_target_pairs={{0,24},{1,25},{2,26},{3,27},{4,28},{5,29},{6,30},{7,31},{8,16},{9,... | collective-permute-start | bytes 208904 | tf_op jit(solution)/shard_map/ppermute | solution.py:723
  325.3 1.6 copy-done.23
  326.9 4.1 %combine_rows.1 = (bf16[1024,512]{1,0:T(8,128)(2,1)}, f32[1,512]{1,0:T(1,128)S(1)}) custom-call(s32[1024,2]{1,0:T(8,128)S(1)} %bitcast.34, bf16[2176,512]{1,0:T(8,128)(2,1)S(1)} %bitcast.31, f32[1024,512]{1,0:T(8,128)S(1)} %copy-done.23), custom_call_target="tpu_custom_call" | custom-call | flops 2281701376 | bytes 8388608 | tf_op jit(solution)/shard_map/combine_rows/pallas_call | solution.py:523
  334.0 2.0 collective-permute-start.13
  337.6 2.1 collective-permute-start.15
  339.7 4.1 %collective-permute-done.15 = bf16[16,2176]{1,0:T(8,128)(2,1)S(1)} collective-permute-done((bf16[16,2176]{1,0:T(8,128)(2,1)S(1)}, bf16[16,2176]{1,0:T(8,128)(2,1)S(1)}, u32[]{:S(2)}, u32[]{:S(2)}) %collective-permute-start.15) | collective-permute-done | bytes 69664 | tf_op jit(solution)/shard_map/ppermute | solution.py:723
  343.8 1.8 collective-permute-done.14
  345.6 2.7 collective-permute-done.16.far_ref
  349.9 1.7 collective-permute-start.19
  351.9 1.6 copy-done.1
  353.5 2.4 grad_sum.1
  355.9 4.3 %collective-permute-done.17 = bf16[64,2176]{1,0:T(8,128)(2,1)S(1)} collective-permute-done((bf16[64,2176]{1,0:T(8,128)(2,1)S(1)}, bf16[64,2176]{1,0:T(8,128)(2,1)S(1)}, u32[]{:S(2)}, u32[]{:S(2)}) %collective-permute-start.17) | collective-permute-done | bytes 278560 | tf_op jit(solution)/shard_map/ppermute | solution.py:723
  363.0 1.5 collective-permute-done.20.far_ref
  364.5 3.0 sums_apart.1
  (122 shorter events, 31.6 us)
Async XLA Ops:
  2.5 15.2 %collective-permute-start = (bf16[2,256,512]{2,1,0:T(8,128)(2,1)}, bf16[2,256,512]{2,1,0:T(8,128)(2,1)}, u32[]{:S(2)}, u32[]{:S(2)}) collective-permute-start(bf16[2,256,512]{2,1,0:T(8,128)(2,1)} %constant_dynamic-slice_fusion), channel_id=1, source_target_pairs={{0,1},{1,0},{2,3},{3,2},{4,5},{5,4},{6,7},{7,6},{8,9},{9,8},{10,11... | collective-permute-start | bytes 1572872 | tf_op jit(solution)/shard_map/ppermute | solution.py:723
  6.2 2.2 copy-start.19
  8.4 15.8 %copy-start.3 = (bf16[512,1536]{0,1:T(8,128)(2,1)}, bf16[512,1536]{0,1:T(8,128)(2,1)S(1)}, u32[]{:S(2)}) copy-start(bf16[512,1536]{0,1:T(8,128)(2,1)S(1)} %copy.35) | copy-start | bytes 4718596
  17.7 6.3 %copy-start.33 = (bf16[512]{0:T(512)(128)(2,1)S(1)}, bf16[512]{0:T(512)(128)(2,1)}, u32[]{:S(2)}) copy-start(bf16[512]{0:T(512)(128)(2,1)} %param.16) | copy-start | bytes 3076
  17.7 6.5 %copy-start.12 = (bf16[4,256,512]{2,1,0:T(8,128)(2,1)S(1)}, bf16[4,256,512]{2,1,0:T(8,128)(2,1)}, u32[]{:S(2)}) copy-start(bf16[4,256,512]{2,1,0:T(8,128)(2,1)} %own_ref.3) | copy-start | bytes 3145732
  17.7 49.8 %all-to-all-start.1 = ((bf16[16,136,512]{2,1,0:T(8,128)(2,1)}), bf16[16,136,512]{2,1,0:T(8,128)(2,1)}, u32[]{:S(2)}, u32[]{:S(2)}) async-start(bf16[16,136,512]{2,1,0:T(8,128)(2,1)} %bitcast.11), calls=%async_computation.1 | async-start | bytes 4456448 | tf_op jit(solution)/shard_map/all_to_all | solution.py:943
  24.1 15.9 %copy-start.14 = (f32[512]{0:T(512)}, f32[512]{0:T(512)S(1)}, u32[]{:S(2)}) copy-start(f32[512]{0:T(512)S(1)} %reshape.112) | copy-start | bytes 6148
  24.2 186.7 %copy-start.15 = (s32[2]{0:T(128)}, s32[2]{0:T(128)S(1)}, u32[]{:S(2)}) copy-start(s32[2]{0:T(128)S(1)} %pad_add_fusion.flag_ref) | copy-start | bytes 28
  24.2 19.6 %copy-start.34 = (bf16[512]{0:T(512)(128)(2,1)S(1)}, bf16[512]{0:T(512)(128)(2,1)}, u32[]{:S(2)}) copy-start(bf16[512]{0:T(512)(128)(2,1)} %param.19) | copy-start | bytes 3076
  24.2 32.2 %copy-start.20 = (bf16[512,512]{1,0:T(8,128)(2,1)S(1)}, bf16[512,512]{1,0:T(8,128)(2,1)}, u32[]{:S(2)}) copy-start(bf16[512,512]{1,0:T(8,128)(2,1)} %w_out_ref.3) | copy-start | bytes 1572868
  39.9 1.7 copy-start.29
  42.2 14.2 %collective-permute-start.1 = (bf16[2,256,512]{2,1,0:T(8,128)(2,1)S(1)}, bf16[2,256,512]{2,1,0:T(8,128)(2,1)S(1)}, u32[]{:S(2)}, u32[]{:S(2)}) collective-permute-start(bf16[2,256,512]{2,1,0:T(8,128)(2,1)S(1)} %get-tuple-element.86), channel_id=1, source_target_pairs={{0,1},{1,0},{2,3},{3,2},{4,5},{5,4},{6,7},{7,6},{8,9},{9,8},{10,11... | collective-permute-start | bytes 1572872 | tf_op jit(solution)/shard_map/ppermute | solution.py:723
  67.5 11.9 %copy-start.13 = (bf16[512,16]{0,1:T(8,128)(2,1)S(1)}, bf16[512,16]{0,1:T(8,128)(2,1)}, u32[]{:S(2)}) copy-start(bf16[512,16]{0,1:T(8,128)(2,1)} %param.20) | copy-start | bytes 49156
  67.5 12.1 %copy-start.31 = (bf16[1,2048]{1,0:T(2,128)(2,1)S(1)}, bf16[1,2048]{1,0:T(2,128)(2,1)}, u32[]{:S(2)}) copy-start(bf16[1,2048]{1,0:T(2,128)(2,1)} %param.22) | copy-start | bytes 12292
  67.5 12.1 %copy-start.32 = (bf16[1,512]{1,0:T(2,128)(2,1)S(1)}, bf16[1,512]{1,0:T(2,128)(2,1)}, u32[]{:S(2)}) copy-start(bf16[1,512]{1,0:T(2,128)(2,1)} %param.24) | copy-start | bytes 3076
  67.5 55.4 %copy-start.17 = (bf16[1,512,2048]{2,1,0:T(8,128)(2,1)S(1)}, bf16[1,512,2048]{2,1,0:T(8,128)(2,1)}, u32[]{:S(2)}) copy-start(bf16[1,512,2048]{2,1,0:T(8,128)(2,1)} %param.21) | copy-start | bytes 6291460
  67.5 55.4 %all-to-all-start = ((bf16[16,136,512]{2,1,0:T(8,128)(2,1)}), bf16[16,136,512]{2,1,0:T(8,128)(2,1)}, u32[]{:S(2)}, u32[]{:S(2)}) async-start(bf16[16,136,512]{2,1,0:T(8,128)(2,1)} %bitcast.9), calls=%async_computation | async-start | bytes 4456448 | tf_op jit(solution)/shard_map/all_to_all | solution.py:943
  122.9 1.6 copy-start.18
  155.7 55.2 %all-to-all-start.2 = ((bf16[16,136,512]{2,1,0:T(8,128)(2,1)}), bf16[16,136,512]{2,1,0:T(8,128)(2,1)}, u32[]{:S(2)}, u32[]{:S(2)}) async-start(bf16[16,136,512]{2,1,0:T(8,128)(2,1)} %bitcast.50), calls=%async_computation.2 | async-start | bytes 4456448 | tf_op jit(solution)/shard_map/all_to_all | solution.py:943
  177.3 65.5 %collective-permute-start.3 = (bf16[512,2048]{1,0:T(8,128)(2,1)}, bf16[512,2048]{1,0:T(8,128)(2,1)}, u32[]{:S(2)}, u32[]{:S(2)}) collective-permute-start(bf16[512,2048]{1,0:T(8,128)(2,1)} %weight_grad.2.own_ref), channel_id=1, source_target_pairs={{0,1},{1,0},{2,3},{3,2},{4,5},{5,4},{6,7},{7,6},{8,9},{9,8},{10,11... | collective-permute-start | bytes 6291464 | tf_op jit(solution)/shard_map/ppermute | solution.py:723
  178.9 32.1 %copy-start.21 = (bf16[512,512]{1,0:T(8,128)(2,1)S(1)}, bf16[512,512]{1,0:T(8,128)(2,1)}, u32[]{:S(2)}) copy-start(bf16[512,512]{1,0:T(8,128)(2,1)} %w_out_ref.3) | copy-start | bytes 1572868
  178.9 32.1 %copy-start.25 = (bf16[1024,512]{1,0:T(8,128)(2,1)S(1)}, bf16[1024,512]{1,0:T(8,128)(2,1)}, u32[]{:S(2)}) copy-start(bf16[1024,512]{1,0:T(8,128)(2,1)} %copy-done.24) | copy-start | bytes 3145732
  226.6 1.8 copy-start.28
  228.4 15.1 %collective-permute-start.2 = (bf16[2,256,512]{2,1,0:T(8,128)(2,1)}, bf16[2,256,512]{2,1,0:T(8,128)(2,1)}, u32[]{:S(2)}, u32[]{:S(2)}) collective-permute-start(bf16[2,256,512]{2,1,0:T(8,128)(2,1)} %bitcast.19), channel_id=1, source_target_pairs={{0,1},{1,0},{2,3},{3,2},{4,5},{5,4},{6,7},{7,6},{8,9},{9,8},{10,11... | collective-permute-start | bytes 1572872 | tf_op jit(solution)/shard_map/ppermute | solution.py:723
  229.9 58.3 %collective-permute-start.4 = (bf16[512,2048]{1,0:T(8,128)(2,1)}, bf16[512,2048]{1,0:T(8,128)(2,1)}, u32[]{:S(2)}, u32[]{:S(2)}) collective-permute-start(bf16[512,2048]{1,0:T(8,128)(2,1)} %weight_grad.3), channel_id=1, source_target_pairs={{0,1},{1,0},{2,3},{3,2},{4,5},{5,4},{6,7},{7,6},{8,9},{9,8},{10,11... | collective-permute-start | bytes 6291464 | tf_op jit(solution)/shard_map/ppermute | solution.py:723
  230.4 83.2 %all-to-all-start.3 = ((bf16[16,136,512]{2,1,0:T(8,128)(2,1)}), bf16[16,136,512]{2,1,0:T(8,128)(2,1)S(1)}, u32[]{:S(2)}, u32[]{:S(2)}) async-start(bf16[16,136,512]{2,1,0:T(8,128)(2,1)} %bitcast.49), calls=%async_computation.3 | async-start | bytes 4456448 | tf_op jit(solution)/shard_map/all_to_all | solution.py:943
  272.5 1.6 copy-start.2
  288.3 3.1 collective-permute-start.5
  288.3 17.1 %collective-permute-start.9 = (f32[1,2560]{1,0:T(1,128)S(1)}, f32[1,2560]{1,0:T(1,128)S(1)}, u32[]{:S(2)}, u32[]{:S(2)}) collective-permute-start(f32[1,2560]{1,0:T(1,128)S(1)} %constant_dynamic-update-slice_fusion), channel_id=1, source_target_pairs={{0,1},{1,0},{2,3},{3,2},{4,5},{5,4},{6,7},{7,6},{8,9},{9,8},{10,11... | collective-permute-start | bytes 30728 | tf_op jit(solution)/shard_map/ppermute | solution.py:723
  291.4 1.6 copy-start
  295.2 10.2 %collective-permute-start.6 = (bf16[64,2176]{1,0:T(8,128)(2,1)S(1)}, bf16[64,2176]{1,0:T(8,128)(2,1)S(1)}, u32[]{:S(2)}, u32[]{:S(2)}) collective-permute-start(bf16[64,2176]{1,0:T(8,128)(2,1)S(1)} %get-tuple-element.117), channel_id=1, source_target_pairs={{0,1},{1,0},{2,3},{3,2},{4,5},{5,4},{6,7},{7,6},{8,9},{9,8},{10,11... | collective-permute-start | bytes 835592 | tf_op jit(solution)/shard_map/ppermute | solution.py:723
  296.8 11.0 %collective-permute-start.7 = (bf16[64,2176]{1,0:T(8,128)(2,1)S(1)}, bf16[64,2176]{1,0:T(8,128)(2,1)S(1)}, u32[]{:S(2)}, u32[]{:S(2)}) collective-permute-start(bf16[64,2176]{1,0:T(8,128)(2,1)S(1)} %get-tuple-element.118), channel_id=1, source_target_pairs={{0,4},{1,5},{2,6},{3,7},{4,0},{5,1},{6,2},{7,3},{8,12},{9,13},{10,... | collective-permute-start | bytes 835592 | tf_op jit(solution)/shard_map/ppermute | solution.py:723
  300.4 12.6 %collective-permute-start.8 = (bf16[64,2176]{1,0:T(8,128)(2,1)S(1)}, bf16[64,2176]{1,0:T(8,128)(2,1)S(1)}, u32[]{:S(2)}, u32[]{:S(2)}) collective-permute-start(bf16[64,2176]{1,0:T(8,128)(2,1)S(1)} %get-tuple-element.119), channel_id=1, source_target_pairs={{0,5},{1,4},{2,7},{3,6},{4,1},{5,0},{6,3},{7,2},{8,13},{9,12},{10,... | collective-permute-start | bytes 835592 | tf_op jit(solution)/shard_map/ppermute | solution.py:723
  317.4 15.5 %collective-permute-start.12 = (bf16[16,2176]{1,0:T(8,128)(2,1)}, bf16[16,2176]{1,0:T(8,128)(2,1)}, u32[]{:S(2)}, u32[]{:S(2)}) collective-permute-start(bf16[16,2176]{1,0:T(8,128)(2,1)} %get-tuple-element.134), channel_id=1, source_target_pairs={{0,24},{1,25},{2,26},{3,27},{4,28},{5,29},{6,30},{7,31},{8,16},{9,... | collective-permute-start | bytes 208904 | tf_op jit(solution)/shard_map/ppermute | solution.py:723
  324.3 8.6 %collective-permute-start.11 = (bf16[16,2176]{1,0:T(8,128)(2,1)}, bf16[16,2176]{1,0:T(8,128)(2,1)}, u32[]{:S(2)}, u32[]{:S(2)}) collective-permute-start(bf16[16,2176]{1,0:T(8,128)(2,1)} %get-tuple-element.133), channel_id=1, source_target_pairs={{0,16},{1,17},{2,18},{3,19},{4,20},{5,21},{6,22},{7,23},{8,24},{9,... | collective-permute-start | bytes 208904 | tf_op jit(solution)/shard_map/ppermute | solution.py:723
  325.3 26.6 %copy-start.4 = (bf16[2,256,512]{2,1,0:T(8,128)(2,1)S(1)}, bf16[2,256,512]{2,1,0:T(8,128)(2,1)}, u32[]{:S(2)}) copy-start(bf16[2,256,512]{2,1,0:T(8,128)(2,1)} %get-tuple-element.140.own_ref) | copy-start | bytes 1572868
  325.3 26.6 %copy-start.16 = (s32[2]{0:T(128)S(1)}, s32[2]{0:T(128)}, u32[]{:S(2)}) copy-start(s32[2]{0:T(128)} %copy-done.15) | copy-start | bytes 28
  325.3 7.7 %collective-permute-start.10 = (bf16[16,2176]{1,0:T(8,128)(2,1)S(1)}, bf16[16,2176]{1,0:T(8,128)(2,1)}, u32[]{:S(2)}, u32[]{:S(2)}) collective-permute-start(bf16[16,2176]{1,0:T(8,128)(2,1)S(1)} %get-tuple-element.132), channel_id=1, source_target_pairs={{0,8},{1,9},{2,10},{3,11},{4,12},{5,13},{6,14},{7,15},{8,0},{9,1},... | collective-permute-start | bytes 208904 | tf_op jit(solution)/shard_map/ppermute | solution.py:723
  325.3 1.6 copy-start.23
  334.0 5.6 %collective-permute-start.13 = (bf16[16,2176]{1,0:T(8,128)(2,1)S(1)}, bf16[16,2176]{1,0:T(8,128)(2,1)S(1)}, u32[]{:S(2)}, u32[]{:S(2)}) collective-permute-start(bf16[16,2176]{1,0:T(8,128)(2,1)S(1)} %select_convert_fusion), channel_id=1, source_target_pairs={{0,8},{1,9},{2,10},{3,11},{4,12},{5,13},{6,14},{7,15},{8,0},{9,1},... | collective-permute-start | bytes 208904 | tf_op jit(solution)/shard_map/ppermute | solution.py:723
  336.1 12.3 %collective-permute-start.16 = (bf16[2,256,512]{2,1,0:T(8,128)(2,1)}, bf16[2,256,512]{2,1,0:T(8,128)(2,1)S(1)}, u32[]{:S(2)}, u32[]{:S(2)}) collective-permute-start(bf16[2,256,512]{2,1,0:T(8,128)(2,1)} %get-tuple-element.135), channel_id=1, source_target_pairs={{0,1},{1,0},{2,3},{3,2},{4,5},{5,4},{6,7},{7,6},{8,9},{9,8},{10,11... | collective-permute-start | bytes 1572872 | tf_op jit(solution)/shard_map/ppermute | solution.py:723
  337.6 6.2 %collective-permute-start.15 = (bf16[16,2176]{1,0:T(8,128)(2,1)S(1)}, bf16[16,2176]{1,0:T(8,128)(2,1)S(1)}, u32[]{:S(2)}, u32[]{:S(2)}) collective-permute-start(bf16[16,2176]{1,0:T(8,128)(2,1)S(1)} %select_convert_fusion), channel_id=1, source_target_pairs={{0,24},{1,25},{2,26},{3,27},{4,28},{5,29},{6,30},{7,31},{8,16},{9,... | collective-permute-start | bytes 208904 | tf_op jit(solution)/shard_map/ppermute | solution.py:723
  339.7 5.9 %collective-permute-start.14 = (bf16[16,2176]{1,0:T(8,128)(2,1)S(1)}, bf16[16,2176]{1,0:T(8,128)(2,1)S(1)}, u32[]{:S(2)}, u32[]{:S(2)}) collective-permute-start(bf16[16,2176]{1,0:T(8,128)(2,1)S(1)} %select_convert_fusion), channel_id=1, source_target_pairs={{0,16},{1,17},{2,18},{3,19},{4,20},{5,21},{6,22},{7,23},{8,24},{9,... | collective-permute-start | bytes 208904 | tf_op jit(solution)/shard_map/ppermute | solution.py:723
  348.4 11.9 %collective-permute-start.17 = (bf16[64,2176]{1,0:T(8,128)(2,1)S(1)}, bf16[64,2176]{1,0:T(8,128)(2,1)S(1)}, u32[]{:S(2)}, u32[]{:S(2)}) collective-permute-start(bf16[64,2176]{1,0:T(8,128)(2,1)S(1)} %maximum_select_fusion.3), channel_id=1, source_target_pairs={{0,1},{1,0},{2,3},{3,2},{4,5},{5,4},{6,7},{7,6},{8,9},{9,8},{10,11... | collective-permute-start | bytes 835592 | tf_op jit(solution)/shard_map/ppermute | solution.py:723
  349.9 10.4 %collective-permute-start.19 = (bf16[64,2176]{1,0:T(8,128)(2,1)S(1)}, bf16[64,2176]{1,0:T(8,128)(2,1)S(1)}, u32[]{:S(2)}, u32[]{:S(2)}) collective-permute-start(bf16[64,2176]{1,0:T(8,128)(2,1)S(1)} %maximum_select_fusion.3), channel_id=1, source_target_pairs={{0,5},{1,4},{2,7},{3,6},{4,1},{5,0},{6,3},{7,2},{8,13},{9,12},{10,... | collective-permute-start | bytes 835592 | tf_op jit(solution)/shard_map/ppermute | solution.py:723
  351.6 9.8 %collective-permute-start.18 = (bf16[64,2176]{1,0:T(8,128)(2,1)S(1)}, bf16[64,2176]{1,0:T(8,128)(2,1)S(1)}, u32[]{:S(2)}, u32[]{:S(2)}) collective-permute-start(bf16[64,2176]{1,0:T(8,128)(2,1)S(1)} %maximum_select_fusion.3), channel_id=1, source_target_pairs={{0,4},{1,5},{2,6},{3,7},{4,0},{5,1},{6,2},{7,3},{8,12},{9,13},{10,... | collective-permute-start | bytes 835592 | tf_op jit(solution)/shard_map/ppermute | solution.py:723
  351.9 1.6 copy-start.1
  361.7 2.8 collective-permute-start.20
  (12 other events, 11.1 us)
